TPU v7x, 512 devices: a whole 4x4x16 slice. The times are simulated.
512 devices in a mesh: ax: 16 (over z), xs: 32 (over x, y, core).
Axes of the slice: x: 4, y: 4, z: 16, core: 2. Of those that a mesh axis runs over, the one named last changes fastest.
Arguments:
- velocity: float32 [3, 128, 1024, 128], P(None, 'ax', 'xs'), may hold values from -6 to 6
- metric: float32 [3, 16, 128, 16], P(None, 'ax', 'xs'), may hold values from 0.05 to 0.3
- bubble_part: int32 [524288], P(('ax', 'xs')), may hold values from 0 to 31, as said below
- bubble_elem: int32 [524288], P(('ax', 'xs')), may hold values from 0 to 63
- bubble_ref: float32 [3, 524288], P(None, ('ax', 'xs')), may hold values from -1 to 1
- bubble_vel: float32 [3, 524288], P(None, ('ax', 'xs')), may hold values from -6 to 6
- inv_tau: float32 [524288], P(('ax', 'xs')), may hold values from 0.5 to 4
- basset_coef: float32 [524288], P(('ax', 'xs')), may hold values from 0.2 to 2
- history: bfloat16 [128, 3, 524288], P(None, None, ('ax', 'xs')), may hold values from -6 to 6
Outputs:
- fluid_rate: float32 [3, 128, 1024, 128], P(None, 'ax', 'xs')
- bubble_rate: float32 [3, 524288], P(None, ('ax', 'xs'))
Inputs may be any that keep to these rules, and one draw needn't show every extreme that they name: `bubble_part`: among the bubbles of one holding device, at most 128 have their element in any one azimuthal sector; in each axial slab one sector holds the elements of exactly 128 bubbles of every device of that slab. `bubble_elem`: the index (ez 4 + ea) * 16 + er of the bubble's element inside its sector and its holder's slab.
All inputs are finite; a program needn't handle non-finite values.
Results may differ from a plain program's by a relative error of at most 0.0046.
Values sent between devices are 32-bit elements; how exact they have to be, the bound alone decides.
A program may use at most 64 MiB of HBM per device.

v0:
```python
import jax
import jax.numpy as jnp
import numpy as np
from jax import lax
from jax.sharding import PartitionSpec as P

GLL_POINTS = (
    -1.0,
    -0.8717401485096066,
    -0.5917001814331423,
    -0.2092992179024789,
    0.2092992179024789,
    0.5917001814331423,
    0.8717401485096066,
    1.0,
)
GLL_WEIGHTS = (
    0.03571428571428571,
    0.21070422714350603,
    0.34112269248350435,
    0.4124587946587039,
    0.4124587946587039,
    0.34112269248350435,
    0.21070422714350603,
    0.03571428571428571,
)


def with_halo(cells, sides, width):
    for axis, dim in sides:
        count = lax.axis_size(axis)
        head = lax.slice_in_dim(cells, 0, width, axis=dim)
        tail = lax.slice_in_dim(cells, cells.shape[dim] - width, cells.shape[dim], axis=dim)
        cells = jnp.concatenate(
            [
                lax.ppermute(tail, axis, [(i, (i + 1) % count) for i in range(count)]),
                cells,
                lax.ppermute(head, axis, [((i + 1) % count, i) for i in range(count)]),
            ],
            axis=dim,
        )
    return cells


def derivative_matrix():
    points = np.array(GLL_POINTS)
    identity = np.eye(8)
    spread = points[:, None] - points[None, :] + identity
    products = np.prod(spread, axis=1)
    matrix = products[:, None] / products[None, :] / spread
    off_diagonal = matrix * (1.0 - identity)
    return off_diagonal - identity * off_diagonal.sum(axis=1)[:, None]


def lagrange_weights(coord):
    columns = []
    for node_index in range(8):
        factor = jnp.ones_like(coord)
        for other_node in range(8):
            if other_node != node_index:
                factor = factor * (
                    (coord - GLL_POINTS[other_node])
                    / (GLL_POINTS[node_index] - GLL_POINTS[other_node])
                )
        columns.append(factor)
    return jnp.stack(columns, axis=0)


def expand_metric(metric):
    return jnp.repeat(jnp.repeat(jnp.repeat(metric, 8, axis=1), 8, axis=2), 8, axis=3)


def advection(velocity, scale):
    matrix = jnp.asarray(derivative_matrix(), jnp.float32)
    comps, zlength, alength, rlength = velocity.shape
    along_z = jnp.einsum(
        "ij,czjar->cziar",
        matrix,
        velocity.reshape(comps, zlength // 8, 8, alength, rlength),
        precision=lax.Precision.HIGHEST,
    ).reshape(velocity.shape)
    along_a = jnp.einsum(
        "ij,czajr->czair",
        matrix,
        velocity.reshape(comps, zlength, alength // 8, 8, rlength),
        precision=lax.Precision.HIGHEST,
    ).reshape(velocity.shape)
    radial_matrix = jnp.asarray(np.kron(np.eye(rlength // 8), derivative_matrix().T), jnp.float32)
    along_r = jnp.dot(velocity, radial_matrix, precision=lax.Precision.HIGHEST)
    return (
        velocity[0:1] * scale[0:1] * along_z
        + velocity[1:2] * scale[1:2] * along_a
        + velocity[2:3] * scale[2:3] * along_r
    )


def nodal_mass(scale):
    weights = np.array(GLL_WEIGHTS)
    zlength, alength, rlength = scale.shape[1:]
    weight_z = jnp.asarray(np.tile(weights, zlength // 8), jnp.float32)
    weight_a = jnp.asarray(np.tile(weights, alength // 8), jnp.float32)
    weight_r = jnp.asarray(np.tile(weights, rlength // 8), jnp.float32)
    return (
        weight_z[:, None, None]
        * weight_a[None, :, None]
        * weight_r[None, None, :]
        / (scale[0] * scale[1] * scale[2])
    )


def pair_local(values, axis_dim, leading):
    length = values.shape[axis_dim]
    zero_plane = jnp.zeros_like(lax.slice_in_dim(values, 0, 1, axis=axis_dim))
    after = jnp.concatenate(
        [lax.slice_in_dim(values, 1, length, axis=axis_dim), zero_plane], axis=axis_dim
    )
    before = jnp.concatenate(
        [zero_plane, lax.slice_in_dim(values, 0, length - 1, axis=axis_dim)], axis=axis_dim
    )
    shape = [1] * values.ndim
    shape[axis_dim] = length
    places = jnp.arange(length).reshape(shape)
    within = (places - leading) % 8
    upper = (within == 7) & (places < length - 1)
    lower = (within == 0) & (places > 0)
    return values + jnp.where(upper, after, 0.0) + jnp.where(lower, before, 0.0)


def quadrature(length):
    steps = jnp.arange(length).astype(jnp.float32)
    return (jnp.sqrt(steps + 1.0) - jnp.sqrt(steps)).astype(jnp.bfloat16)


def element_table(source):
    fields, zlength, alength, rlength = source.shape
    blocks = source.reshape(fields, zlength // 8, 8, alength // 8, 8, rlength // 8, 8)
    return blocks.transpose(1, 3, 5, 0, 2, 4, 6).reshape(-1, fields * 512)


def interpolate(table, coords, element_value):
    element = element_value.astype(jnp.int32)
    batch, slots = element.shape
    fields = table.shape[1] // 512
    rows = jnp.take(table, element.reshape(-1), axis=0).reshape(batch, slots, fields, 8, 8, 8)
    lag_z = lagrange_weights(coords[:, 0]).astype(jnp.bfloat16)
    lag_a = lagrange_weights(coords[:, 1]).astype(jnp.bfloat16)
    lag_r = lagrange_weights(coords[:, 2]).astype(jnp.bfloat16)
    first = jnp.einsum("bsczar,rbs->bscza", rows, lag_r, preferred_element_type=jnp.float32)
    second = jnp.einsum(
        "bscza,abs->bscz", first, lag_a.astype(jnp.float32), precision=lax.Precision.HIGHEST
    )
    return jnp.einsum(
        "bscz,zbs->bcs", second, lag_z.astype(jnp.float32), precision=lax.Precision.HIGHEST
    )


def grouped(received, handler):
    sources, width, items = received.shape
    blocks = received.reshape(sources // 4, 4, width, items)
    result = lax.map(handler, blocks)
    return result.reshape(sources, result.shape[2], items)


def shards(
    velocity,
    metric,
    bubble_part,
    bubble_elem,
    bubble_ref,
    bubble_vel,
    inv_tau,
    basset_coef,
    history,
):
    scale = expand_metric(metric)
    advect = advection(velocity, scale)
    mass = nodal_mass(scale)
    weighted = jnp.concatenate([mass[None] * advect, mass[None]], axis=0)
    radial = pair_local(weighted, 3, 0)
    padded = with_halo(radial, (("xs", 2),), 1)
    across = pair_local(padded, 2, 1)[:, :, 1:-1]
    padded_axial = with_halo(across, (("ax", 1),), 1)
    summed = pair_local(padded_axial, 1, 1)[:, 1:-1]
    fluid_rate = -summed[0:3] / summed[3:4]
    source = jnp.concatenate([velocity, advect], axis=0).astype(jnp.bfloat16)
    table = element_table(source)
    held_count = bubble_part.shape[0]
    quad = quadrature(history.shape[0])
    basset = basset_coef[None] * jnp.dot(
        quad, history.reshape(history.shape[0], -1), preferred_element_type=jnp.float32
    ).reshape(3, held_count)
    sectors = lax.axis_size("xs")
    capacity = held_count * 4 // sectors
    onehot = (bubble_part[:, None] == jnp.arange(sectors)[None, :]).astype(jnp.int32)
    ranks = jnp.sum((jnp.cumsum(onehot, axis=0) - 1) * onehot, axis=1)
    element_value = bubble_elem.astype(jnp.float32)[None]
    query = jnp.concatenate([bubble_ref, element_value], axis=0)
    outgoing = (
        jnp.zeros((sectors, query.shape[0], capacity), jnp.float32)
        .at[bubble_part, :, ranks]
        .set(query.T)
    )

    def probe_handler(block):
        return interpolate(table, block[:, 0:3], block[:, 3])

    answers = grouped(
        lax.all_to_all(outgoing, "xs", split_axis=0, concat_axis=0, tiled=True), probe_handler
    )
    returned = lax.all_to_all(answers, "xs", split_axis=0, concat_axis=0, tiled=True)
    probe = returned[bubble_part, :, ranks].T
    bubble_rate = 3.0 * probe[3:6] + inv_tau[None] * (probe[0:3] - bubble_vel) + basset
    return (fluid_rate, bubble_rate)


def solution(mesh):
    return jax.shard_map(
        shards,
        mesh=mesh,
        in_specs=(
            P(None, "ax", "xs", None),
            P(None, "ax", "xs", None),
            P(("ax", "xs")),
            P(("ax", "xs")),
            P(None, ("ax", "xs")),
            P(None, ("ax", "xs")),
            P(("ax", "xs")),
            P(("ax", "xs")),
            P(None, None, ("ax", "xs")),
        ),
        out_specs=(P(None, "ax", "xs", None), P(None, ("ax", "xs"))),
        check_vma=False,
    )
```

profile of v0, /device:TPU:1, one launch (start us, length us, event | category | flops | bytes accessed | tf_op | source)
XLA Modules:
  0.0 237.1 jit_solution(15146932299207101150)
XLA Ops:
  10.7 4.6 %collective-permute-start = (f32[4,8,1,128]{3,1,2,0:T(8,128)}, f32[4,8,1,128]{3,1,2,0:T(8,128)}, u32[]{:S(2)}, u32[]{:S(2)}) collective-permute-start(f32[4,8,1,128]{3,1,2,0:T(8,128)} %get-tuple-element.177), channel_id=1, source_target_pairs={{0,1},{1,2},{2,3},{3,4},{4,5},{5,6},{6,7},{7,8},{8,9},{9,10},{10,1... | collective-permute-start | bytes 49160 | tf_op jit(solution)/shard_map/ppermute | solution.py:36
  15.2 6.1 %collective-permute-start.1 = (f32[4,8,1,128]{3,1,2,0:T(8,128)}, f32[4,8,1,128]{3,1,2,0:T(8,128)}, u32[]{:S(2)}, u32[]{:S(2)}) collective-permute-start(f32[4,8,1,128]{3,1,2,0:T(8,128)} %get-tuple-element.176), channel_id=1, source_target_pairs={{1,0},{2,1},{3,2},{4,3},{5,4},{6,5},{7,6},{8,7},{9,8},{10,9},{11,1... | collective-permute-start | bytes 49160 | tf_op jit(solution)/shard_map/ppermute | solution.py:38
  21.4 9.0 %reduce-window.6 = s32[32,8,128]{2,1,0:T(8,128)S(1)} reduce-window(s32[32,8,128]{2,1,0:T(8,128)S(1)} %fusion.27, s32[]{:T(128)} %copy.310), window={size=1x1x128 pad=0_0x0_0x127_0}, to_apply=%region_0.1 | reduce-window | flops 4161536 | bytes 262148 | tf_op jit(solution)/shard_map/reduce-window
  31.4 3.6 %scatter_custom_fusion = f32[4096,4]{1,0:T(8,128)S(1)} fusion(s32[1024]{0:T(1024)S(1)} %broadcast_select_fusion, f32[1024,4]{1,0:T(8,128)S(1)} %copy.213, f32[]{:T(128)} %constant.674.clone.1), kind=kCustom, calls=%fused_computation.106 | custom fusion | bytes 65540
  36.3 9.2 %all-to-all-start = ((f32[32,4,128]{2,1,0:T(4,128)}), f32[32,4,128]{2,1,0:T(4,128)}, u32[]{:S(2)}, u32[]{:S(2)}) async-start(f32[32,4,128]{2,1,0:T(4,128)} %bitcast.72), calls=%async_computation | async-start | bytes 131072 | tf_op jit(solution)/shard_map/all_to_all | solution.py:208
  45.6 3.6 %concatenate.77 = bf16[3,1,8,4,8,16,8]{6,5,4,3,2,0,1:T(8,128)(2,1)S(1)} reshape(bf16[3,8,32,128]{3,2,1,0:T(8,128)(2,1)S(1)} %copy.216) | data formatting | bytes 393216 | tf_op jit(solution)/shard_map/concatenate | solution.py:185
  49.2 4.6 %concatenate.76 = bf16[3,1,8,4,8,16,8]{6,5,4,3,2,0,1:T(8,128)(2,1)} reshape(bf16[3,8,32,128]{3,2,1,0:T(8,128)(2,1)S(1)} %convert.80) | data formatting | bytes 393216 | tf_op jit(solution)/shard_map/concatenate | solution.py:185
  58.2 5.7 %maximum_bitcast_fusion = bf16[1,4,16,6,8,8,8]{6,2,5,1,4,3,0:T(8,128)(2,1)} fusion(bf16[3,1,8,4,8,16,8]{6,5,4,3,2,0,1:T(8,128)(2,1)S(1)} %concatenate.77, bf16[3,1,8,4,8,16,8]{6,5,4,3,2,0,1:T(8,128)(2,1)} %concatenate.76), kind=kLoop, calls=%fused_computation.90 | loop fusion | flops 196608 | bytes 786432 | tf_op jit(solution)/shard_map/transpose | solution.py:137
  64.5 6.5 %copy.217 = bf16[1,4,16,6,8,8,8]{2,1,6,5,4,3,0:T(4,128)(2,1)S(1)} copy(bf16[1,4,16,6,8,8,8]{6,2,5,1,4,3,0:T(8,128)(2,1)} %maximum_bitcast_fusion) | data formatting | bytes 786432 | tf_op jit(solution)/shard_map/transpose | solution.py:137
  80.1 5.9 %collective-permute-start.3 = (f32[4,1,32,128]{3,1,2,0:T(1,128)}, f32[4,1,32,128]{3,1,2,0:T(1,128)}, u32[]{:S(2)}, u32[]{:S(2)}) collective-permute-start(f32[4,1,32,128]{3,1,2,0:T(1,128)} %get-tuple-element.174), channel_id=1, source_target_pairs={{32,0},{64,32},{96,64},{128,96},{160,128},{192,160},{224,192},{256... | collective-permute-start | bytes 196616 | tf_op jit(solution)/shard_map/ppermute | solution.py:38
  86.0 127.3 %while.13 = (s32[]{:T(128)}, f32[8,4,6,128]{3,2,1,0:T(8,128)}, f32[8,4,4,128]{3,2,1,0:T(4,128)}, bf16[64,3072]{1,0:T(8,128)(2,1)S(1)}, s32[]{:T(128)}) while((s32[]{:T(128)}, f32[8,4,6,128]{3,2,1,0:T(8,128)}, f32[8,4,4,128]{3,2,1,0:T(4,128)}, bf16[64,3072]{1,0:T(8,128)(2,1)S(1)}, s32[]{:T(128)}) %tuple.70), condition=%wide.region_5.6_spmd, body=%wide.region_4.5_spmd.sunk | while | flops 6786559 | bytes 24276656 | solution.py:160
  87.7 2.9 %gather_fusion = bf16[512,3072]{1,0:T(8,128)(2,1)S(1)} fusion(bf16[64,3072]{1,0:T(8,128)(2,1)S(1)} %get-tuple-element.252, s32[1024]{0:T(1024)S(1)} %pad_clamp_fusion.2), kind=kCustom, calls=%fused_computation.clone.1 | custom fusion | bytes 6293504 | tf_op jit(solution)/shard_map/while/body/eval_jaxpr/jit(_take)/gather | solution.py:144
  93.5 3.8 %gather.20 = bf16[4,128,6,8,8,8]{1,0,5,4,3,2:T(4,128)(2,1)S(1)} reshape(bf16[512,3072]{0,1:T(8,128)(2,1)} %copy.278) | data formatting | bytes 6291456 | tf_op jit(solution)/shard_map/while/body/eval_jaxpr/jit(_take)/gather | solution.py:144
  97.3 3.7 %multiply_reduce_fusion.5 = f32[4,128,6,8,8]{1,0,4,3,2:T(4,128)S(1)} fusion(f32[4,128,8]{1,0,2:T(4,128)} %bitcast_convert_fusion.6, bf16[4,128,6,8,8,8]{1,0,5,4,3,2:T(4,128)(2,1)S(1)} %gather.20, pred[4,128]{1,0:T(4,128)(4,1)S(1)} %compare_and_fusion.8), kind=kLoop, calls=%fused_computation.3.clone.1 | loop fusion | flops 6094848 | bytes 3949056 | tf_op jit(solution)/shard_map/while
  109.4 3.8 %gather.20 = bf16[4,128,6,8,8,8]{1,0,5,4,3,2:T(4,128)(2,1)S(1)} reshape(bf16[512,3072]{0,1:T(8,128)(2,1)} %copy.278) | data formatting | bytes 6291456 | tf_op jit(solution)/shard_map/while/body/eval_jaxpr/jit(_take)/gather | solution.py:144
  113.2 3.7 %multiply_reduce_fusion.5 = f32[4,128,6,8,8]{1,0,4,3,2:T(4,128)S(1)} fusion(f32[4,128,8]{1,0,2:T(4,128)} %bitcast_convert_fusion.6, bf16[4,128,6,8,8,8]{1,0,5,4,3,2:T(4,128)(2,1)S(1)} %gather.20, pred[4,128]{1,0:T(4,128)(4,1)S(1)} %compare_and_fusion.8), kind=kLoop, calls=%fused_computation.3.clone.1 | loop fusion | flops 6094848 | bytes 3949056 | tf_op jit(solution)/shard_map/while
  125.3 3.8 %gather.20 = bf16[4,128,6,8,8,8]{1,0,5,4,3,2:T(4,128)(2,1)S(1)} reshape(bf16[512,3072]{0,1:T(8,128)(2,1)} %copy.278) | data formatting | bytes 6291456 | tf_op jit(solution)/shard_map/while/body/eval_jaxpr/jit(_take)/gather | solution.py:144
  129.1 3.7 %multiply_reduce_fusion.5 = f32[4,128,6,8,8]{1,0,4,3,2:T(4,128)S(1)} fusion(f32[4,128,8]{1,0,2:T(4,128)} %bitcast_convert_fusion.6, bf16[4,128,6,8,8,8]{1,0,5,4,3,2:T(4,128)(2,1)S(1)} %gather.20, pred[4,128]{1,0:T(4,128)(4,1)S(1)} %compare_and_fusion.8), kind=kLoop, calls=%fused_computation.3.clone.1 | loop fusion | flops 6094848 | bytes 3949056 | tf_op jit(solution)/shard_map/while
  141.2 3.8 %gather.20 = bf16[4,128,6,8,8,8]{1,0,5,4,3,2:T(4,128)(2,1)S(1)} reshape(bf16[512,3072]{0,1:T(8,128)(2,1)} %copy.278) | data formatting | bytes 6291456 | tf_op jit(solution)/shard_map/while/body/eval_jaxpr/jit(_take)/gather | solution.py:144
  145.0 3.7 %multiply_reduce_fusion.5 = f32[4,128,6,8,8]{1,0,4,3,2:T(4,128)S(1)} fusion(f32[4,128,8]{1,0,2:T(4,128)} %bitcast_convert_fusion.6, bf16[4,128,6,8,8,8]{1,0,5,4,3,2:T(4,128)(2,1)S(1)} %gather.20, pred[4,128]{1,0:T(4,128)(4,1)S(1)} %compare_and_fusion.8), kind=kLoop, calls=%fused_computation.3.clone.1 | loop fusion | flops 6094848 | bytes 3949056 | tf_op jit(solution)/shard_map/while
  157.1 3.8 %gather.20 = bf16[4,128,6,8,8,8]{1,0,5,4,3,2:T(4,128)(2,1)S(1)} reshape(bf16[512,3072]{0,1:T(8,128)(2,1)} %copy.278) | data formatting | bytes 6291456 | tf_op jit(solution)/shard_map/while/body/eval_jaxpr/jit(_take)/gather | solution.py:144
  160.9 3.7 %multiply_reduce_fusion.5 = f32[4,128,6,8,8]{1,0,4,3,2:T(4,128)S(1)} fusion(f32[4,128,8]{1,0,2:T(4,128)} %bitcast_convert_fusion.6, bf16[4,128,6,8,8,8]{1,0,5,4,3,2:T(4,128)(2,1)S(1)} %gather.20, pred[4,128]{1,0:T(4,128)(4,1)S(1)} %compare_and_fusion.8), kind=kLoop, calls=%fused_computation.3.clone.1 | loop fusion | flops 6094848 | bytes 3949056 | tf_op jit(solution)/shard_map/while
  167.3 2.9 %gather_fusion = bf16[512,3072]{1,0:T(8,128)(2,1)S(1)} fusion(bf16[64,3072]{1,0:T(8,128)(2,1)S(1)} %get-tuple-element.252, s32[1024]{0:T(1024)S(1)} %pad_clamp_fusion.2), kind=kCustom, calls=%fused_computation.clone.1 | custom fusion | bytes 6293504 | tf_op jit(solution)/shard_map/while/body/eval_jaxpr/jit(_take)/gather | solution.py:144
  173.1 3.8 %gather.20 = bf16[4,128,6,8,8,8]{1,0,5,4,3,2:T(4,128)(2,1)S(1)} reshape(bf16[512,3072]{0,1:T(8,128)(2,1)} %copy.278) | data formatting | bytes 6291456 | tf_op jit(solution)/shard_map/while/body/eval_jaxpr/jit(_take)/gather | solution.py:144
  176.9 3.7 %multiply_reduce_fusion.5 = f32[4,128,6,8,8]{1,0,4,3,2:T(4,128)S(1)} fusion(f32[4,128,8]{1,0,2:T(4,128)} %bitcast_convert_fusion.6, bf16[4,128,6,8,8,8]{1,0,5,4,3,2:T(4,128)(2,1)S(1)} %gather.20, pred[4,128]{1,0:T(4,128)(4,1)S(1)} %compare_and_fusion.8), kind=kLoop, calls=%fused_computation.3.clone.1 | loop fusion | flops 6094848 | bytes 3949056 | tf_op jit(solution)/shard_map/while
  189.0 3.8 %gather.20 = bf16[4,128,6,8,8,8]{1,0,5,4,3,2:T(4,128)(2,1)S(1)} reshape(bf16[512,3072]{0,1:T(8,128)(2,1)} %copy.278) | data formatting | bytes 6291456 | tf_op jit(solution)/shard_map/while/body/eval_jaxpr/jit(_take)/gather | solution.py:144
  192.8 3.7 %multiply_reduce_fusion.5 = f32[4,128,6,8,8]{1,0,4,3,2:T(4,128)S(1)} fusion(f32[4,128,8]{1,0,2:T(4,128)} %bitcast_convert_fusion.6, bf16[4,128,6,8,8,8]{1,0,5,4,3,2:T(4,128)(2,1)S(1)} %gather.20, pred[4,128]{1,0:T(4,128)(4,1)S(1)} %compare_and_fusion.8), kind=kLoop, calls=%fused_computation.3.clone.1 | loop fusion | flops 6094848 | bytes 3949056 | tf_op jit(solution)/shard_map/while
  204.9 3.8 %gather.20 = bf16[4,128,6,8,8,8]{1,0,5,4,3,2:T(4,128)(2,1)S(1)} reshape(bf16[512,3072]{0,1:T(8,128)(2,1)} %copy.278) | data formatting | bytes 6291456 | tf_op jit(solution)/shard_map/while/body/eval_jaxpr/jit(_take)/gather | solution.py:144
  208.7 3.7 %multiply_reduce_fusion.5 = f32[4,128,6,8,8]{1,0,4,3,2:T(4,128)S(1)} fusion(f32[4,128,8]{1,0,2:T(4,128)} %bitcast_convert_fusion.6, bf16[4,128,6,8,8,8]{1,0,5,4,3,2:T(4,128)(2,1)S(1)} %gather.20, pred[4,128]{1,0:T(4,128)(4,1)S(1)} %compare_and_fusion.8), kind=kLoop, calls=%fused_computation.3.clone.1 | loop fusion | flops 6094848 | bytes 3949056 | tf_op jit(solution)/shard_map/while
  213.3 7.8 %all-to-all-start.1 = ((f32[32,6,128]{2,1,0:T(8,128)}), f32[32,6,128]{2,1,0:T(8,128)S(1)}, u32[]{:S(2)}, u32[]{:S(2)}) async-start(f32[32,6,128]{2,1,0:T(8,128)} %bitcast.75), calls=%async_computation.1 | async-start | bytes 262144 | tf_op jit(solution)/shard_map/all_to_all | solution.py:210
  224.1 4.7 %all-to-all-done.1 = f32[32,6,128]{2,1,0:T(8,128)S(1)} async-done(((f32[32,6,128]{2,1,0:T(8,128)}), f32[32,6,128]{2,1,0:T(8,128)S(1)}, u32[]{:S(2)}, u32[]{:S(2)}) %all-to-all-start.1) | async-done | bytes 98336 | tf_op jit(solution)/shard_map/all_to_all | solution.py:210
  229.5 6.8 %gather_fusion.1 = f32[1024,6]{1,0:T(8,128)S(1)} fusion(f32[32,6,128]{1,2,0:T(8,128)S(1)} %copy.220, s32[1024]{0:T(1024)S(1)} %bitcast.251), kind=kCustom, calls=%fused_computation.1 | custom fusion | bytes 57344 | tf_op jit(solution)/shard_map/gather | solution.py:211
  (439 shorter events, 91.4 us)
Async XLA Ops:
  0.6 6.7 %copy-start.16 = (f32[128,128,1,1]{1,0,3,2:T(8,128)S(1)}, f32[128,128,1,1]{1,0,3,2:T(8,128)}, u32[]{:S(2)}) copy-start(f32[128,128,1,1]{1,0,3,2:T(8,128)} %constant.727) | copy-start | bytes 196612
  0.6 7.4 %copy-start.10 = (f32[8,8,1,1]{1,0,3,2:T(8,128)S(1)}, f32[8,8,1,1]{1,0,3,2:T(8,128)}, u32[]{:S(2)}) copy-start(f32[8,8,1,1]{1,0,3,2:T(8,128)} %constant.725) | copy-start | bytes 772
  0.7 6.7 %copy-start = (f32[3,8,32,128]{3,2,1,0:T(8,128)S(1)}, f32[3,8,32,128]{3,2,1,0:T(8,128)}, u32[]{:S(2)}) copy-start(f32[3,8,32,128]{3,2,1,0:T(8,128)} %param.16) | copy-start | bytes 1179652
  8.0 13.4 %copy-start.7 = (s32[1024]{0:T(1024)S(1)}, s32[1024]{0:T(1024)}, u32[]{:S(2)}) copy-start(s32[1024]{0:T(1024)} %param.18) | copy-start | bytes 12292
  8.0 23.0 %copy-start.15 = (s32[2]{0:T(128)S(1)}, s32[2]{0:T(128)}, u32[]{:S(2)}) copy-start(s32[2]{0:T(128)} %constant.701) | copy-start | bytes 28
  8.0 23.0 %copy-start.14 = (s32[2]{0:T(128)S(1)}, s32[2]{0:T(128)}, u32[]{:S(2)}) copy-start(s32[2]{0:T(128)} %constant.704) | copy-start | bytes 28
  8.0 23.1 %copy-start.11 = (s32[1024]{0:T(1024)S(1)}, s32[1024]{0:T(1024)}, u32[]{:S(2)}) copy-start(s32[1024]{0:T(1024)} %param.19) | copy-start | bytes 12292
  8.0 23.1 %copy-start.8 = (f32[3,1024]{1,0:T(4,128)S(1)}, f32[3,1024]{1,0:T(4,128)}, u32[]{:S(2)}) copy-start(f32[3,1024]{1,0:T(4,128)} %param.20) | copy-start | bytes 36868
  10.7 64.3 %collective-permute-start = (f32[4,8,1,128]{3,1,2,0:T(8,128)}, f32[4,8,1,128]{3,1,2,0:T(8,128)}, u32[]{:S(2)}, u32[]{:S(2)}) collective-permute-start(f32[4,8,1,128]{3,1,2,0:T(8,128)} %get-tuple-element.177), channel_id=1, source_target_pairs={{0,1},{1,2},{2,3},{3,4},{4,5},{5,6},{6,7},{7,8},{8,9},{9,10},{10,1... | collective-permute-start | bytes 49160 | tf_op jit(solution)/shard_map/ppermute | solution.py:36
  15.2 59.7 %collective-permute-start.1 = (f32[4,8,1,128]{3,1,2,0:T(8,128)}, f32[4,8,1,128]{3,1,2,0:T(8,128)}, u32[]{:S(2)}, u32[]{:S(2)}) collective-permute-start(f32[4,8,1,128]{3,1,2,0:T(8,128)} %get-tuple-element.176), channel_id=1, source_target_pairs={{1,0},{2,1},{3,2},{4,3},{5,4},{6,5},{7,6},{8,7},{9,8},{10,9},{11,1... | collective-permute-start | bytes 49160 | tf_op jit(solution)/shard_map/ppermute | solution.py:38
  36.3 49.7 %all-to-all-start = ((f32[32,4,128]{2,1,0:T(4,128)}), f32[32,4,128]{2,1,0:T(4,128)}, u32[]{:S(2)}, u32[]{:S(2)}) async-start(f32[32,4,128]{2,1,0:T(4,128)} %bitcast.72), calls=%async_computation | async-start | bytes 131072 | tf_op jit(solution)/shard_map/all_to_all | solution.py:208
  78.1 143.0 %collective-permute-start.2 = (f32[4,1,32,128]{3,1,2,0:T(1,128)}, f32[4,1,32,128]{3,1,2,0:T(1,128)}, u32[]{:S(2)}, u32[]{:S(2)}) collective-permute-start(f32[4,1,32,128]{3,1,2,0:T(1,128)} %get-tuple-element.175), channel_id=1, source_target_pairs={{0,32},{32,64},{64,96},{96,128},{128,160},{160,192},{192,224},{224... | collective-permute-start | bytes 196616 | tf_op jit(solution)/shard_map/ppermute | solution.py:36
  80.1 141.1 %collective-permute-start.3 = (f32[4,1,32,128]{3,1,2,0:T(1,128)}, f32[4,1,32,128]{3,1,2,0:T(1,128)}, u32[]{:S(2)}, u32[]{:S(2)}) collective-permute-start(f32[4,1,32,128]{3,1,2,0:T(1,128)} %get-tuple-element.174), channel_id=1, source_target_pairs={{32,0},{64,32},{96,64},{128,96},{160,128},{192,160},{224,192},{256... | collective-permute-start | bytes 196616 | tf_op jit(solution)/shard_map/ppermute | solution.py:38
  97.3 3.7 %copy-start.3 = (bf16[8,4,128]{2,1,0:T(4,128)(2,1)S(1)}, bf16[8,4,128]{2,1,0:T(4,128)(2,1)}, u32[]{:S(2)}) copy-start(bf16[8,4,128]{2,1,0:T(4,128)(2,1)} %copy-done.2) | copy-start | bytes 24580 | tf_op jit(solution)/shard_map/while
  97.3 4.0 %copy-start.5 = (bf16[8,4,128]{2,1,0:T(4,128)(2,1)S(1)}, bf16[8,4,128]{2,1,0:T(4,128)(2,1)}, u32[]{:S(2)}) copy-start(bf16[8,4,128]{2,1,0:T(4,128)(2,1)} %copy-done.4) | copy-start | bytes 24580 | tf_op jit(solution)/shard_map/while
  113.2 3.7 %copy-start.3 = (bf16[8,4,128]{2,1,0:T(4,128)(2,1)S(1)}, bf16[8,4,128]{2,1,0:T(4,128)(2,1)}, u32[]{:S(2)}) copy-start(bf16[8,4,128]{2,1,0:T(4,128)(2,1)} %copy-done.2) | copy-start | bytes 24580 | tf_op jit(solution)/shard_map/while
  113.2 4.0 %copy-start.5 = (bf16[8,4,128]{2,1,0:T(4,128)(2,1)S(1)}, bf16[8,4,128]{2,1,0:T(4,128)(2,1)}, u32[]{:S(2)}) copy-start(bf16[8,4,128]{2,1,0:T(4,128)(2,1)} %copy-done.4) | copy-start | bytes 24580 | tf_op jit(solution)/shard_map/while
  129.1 3.7 %copy-start.3 = (bf16[8,4,128]{2,1,0:T(4,128)(2,1)S(1)}, bf16[8,4,128]{2,1,0:T(4,128)(2,1)}, u32[]{:S(2)}) copy-start(bf16[8,4,128]{2,1,0:T(4,128)(2,1)} %copy-done.2) | copy-start | bytes 24580 | tf_op jit(solution)/shard_map/while
  129.1 4.0 %copy-start.5 = (bf16[8,4,128]{2,1,0:T(4,128)(2,1)S(1)}, bf16[8,4,128]{2,1,0:T(4,128)(2,1)}, u32[]{:S(2)}) copy-start(bf16[8,4,128]{2,1,0:T(4,128)(2,1)} %copy-done.4) | copy-start | bytes 24580 | tf_op jit(solution)/shard_map/while
  145.0 3.7 %copy-start.3 = (bf16[8,4,128]{2,1,0:T(4,128)(2,1)S(1)}, bf16[8,4,128]{2,1,0:T(4,128)(2,1)}, u32[]{:S(2)}) copy-start(bf16[8,4,128]{2,1,0:T(4,128)(2,1)} %copy-done.2) | copy-start | bytes 24580 | tf_op jit(solution)/shard_map/while
  145.0 4.0 %copy-start.5 = (bf16[8,4,128]{2,1,0:T(4,128)(2,1)S(1)}, bf16[8,4,128]{2,1,0:T(4,128)(2,1)}, u32[]{:S(2)}) copy-start(bf16[8,4,128]{2,1,0:T(4,128)(2,1)} %copy-done.4) | copy-start | bytes 24580 | tf_op jit(solution)/shard_map/while
  160.9 3.7 %copy-start.3 = (bf16[8,4,128]{2,1,0:T(4,128)(2,1)S(1)}, bf16[8,4,128]{2,1,0:T(4,128)(2,1)}, u32[]{:S(2)}) copy-start(bf16[8,4,128]{2,1,0:T(4,128)(2,1)} %copy-done.2) | copy-start | bytes 24580 | tf_op jit(solution)/shard_map/while
  160.9 4.0 %copy-start.5 = (bf16[8,4,128]{2,1,0:T(4,128)(2,1)S(1)}, bf16[8,4,128]{2,1,0:T(4,128)(2,1)}, u32[]{:S(2)}) copy-start(bf16[8,4,128]{2,1,0:T(4,128)(2,1)} %copy-done.4) | copy-start | bytes 24580 | tf_op jit(solution)/shard_map/while
  176.8 3.7 %copy-start.3 = (bf16[8,4,128]{2,1,0:T(4,128)(2,1)S(1)}, bf16[8,4,128]{2,1,0:T(4,128)(2,1)}, u32[]{:S(2)}) copy-start(bf16[8,4,128]{2,1,0:T(4,128)(2,1)} %copy-done.2) | copy-start | bytes 24580 | tf_op jit(solution)/shard_map/while
  176.8 4.0 %copy-start.5 = (bf16[8,4,128]{2,1,0:T(4,128)(2,1)S(1)}, bf16[8,4,128]{2,1,0:T(4,128)(2,1)}, u32[]{:S(2)}) copy-start(bf16[8,4,128]{2,1,0:T(4,128)(2,1)} %copy-done.4) | copy-start | bytes 24580 | tf_op jit(solution)/shard_map/while
  192.7 4.0 %copy-start.5 = (bf16[8,4,128]{2,1,0:T(4,128)(2,1)S(1)}, bf16[8,4,128]{2,1,0:T(4,128)(2,1)}, u32[]{:S(2)}) copy-start(bf16[8,4,128]{2,1,0:T(4,128)(2,1)} %copy-done.4) | copy-start | bytes 24580 | tf_op jit(solution)/shard_map/while
  208.6 4.0 %copy-start.5 = (bf16[8,4,128]{2,1,0:T(4,128)(2,1)S(1)}, bf16[8,4,128]{2,1,0:T(4,128)(2,1)}, u32[]{:S(2)}) copy-start(bf16[8,4,128]{2,1,0:T(4,128)(2,1)} %copy-done.4) | copy-start | bytes 24580 | tf_op jit(solution)/shard_map/while
  213.3 15.5 %all-to-all-start.1 = ((f32[32,6,128]{2,1,0:T(8,128)}), f32[32,6,128]{2,1,0:T(8,128)S(1)}, u32[]{:S(2)}, u32[]{:S(2)}) async-start(f32[32,6,128]{2,1,0:T(8,128)} %bitcast.75), calls=%async_computation.1 | async-start | bytes 262144 | tf_op jit(solution)/shard_map/all_to_all | solution.py:210
  229.4 7.0 %copy-start.6 = (f32[1,3,1024]{2,0,1:T(1,128)S(1)}, f32[1,3,1024]{2,0,1:T(1,128)}, u32[]{:S(2)}) copy-start(f32[1,3,1024]{2,0,1:T(1,128)} %fusion.11) | copy-start | bytes 36868
  229.4 7.0 %copy-start.9 = (f32[3,1024]{1,0:T(4,128)S(1)}, f32[3,1024]{1,0:T(4,128)}, u32[]{:S(2)}) copy-start(f32[3,1024]{1,0:T(4,128)} %param.21) | copy-start | bytes 36868
  229.5 7.0 %copy-start.12 = (f32[1024]{0:T(1024)S(1)}, f32[1024]{0:T(1024)}, u32[]{:S(2)}) copy-start(f32[1024]{0:T(1024)} %param.23) | copy-start | bytes 12292
  229.5 7.0 %copy-start.13 = (f32[1024]{0:T(1024)S(1)}, f32[1024]{0:T(1024)}, u32[]{:S(2)}) copy-start(f32[1024]{0:T(1024)} %param.22) | copy-start | bytes 12292
  (19 other events, 21.0 us)
where the time goes:
time: 239 us; the launch traced here: 237 us
  local copies, waits for them, and re-layouts  126 us (53%)
  other arithmetic  63.5 us (27%)
  starting transfers between devices  35.5 us (15%)
  matrix products  4.88 us (2%)
  waiting for transfers between devices  4.7 us (2%)
    gather x24, local copies, waits for them, and re-layouts, interpolate(): jnp.take(table, element.reshape(-1), axis=0)  76 us
    while x160, other arithmetic  36.6 us
    ppermute x2, starting transfers between devices, with_halo(): lax.ppermute(head, axis, [((i + 1) % count, i) for i in range(count)])  12 us
    all_to_all x1, starting transfers between devices, shards(): lax.all_to_all(outgoing, 'xs', split_axis=0, concat_axis=0, tiled=True)  9.2 us
    another operation x3, other arithmetic  9.07 us
    unnamed x30, local copies, waits for them, and re-layouts  8.84 us
    concatenate x2, local copies, waits for them, and re-layouts, shards(): source = jnp.concatenate([velocity, advect], axis=0).astype(jnp.bfloat16)  8.22 us
    all_to_all x1, starting transfers between devices, shards(): lax.all_to_all(answers, 'xs', split_axis=0, concat_axis=0, tiled=True)  7.77 us
  transfers between devices with their start and end apart: 6, of which 1 were waited for; matrix products, arithmetic and copies ran while one was open for 74% of the time, Pallas kernels for 0%

commit v1 on v0

v1 whole, which is shorter than its diff:
```python
import functools

import jax
import jax.numpy as jnp
import numpy as np
from jax import lax
from jax.experimental import pallas as pl
from jax.experimental.pallas import tpu as pltpu
from jax.sharding import PartitionSpec as P

GLL_POINTS = (
    -1.0,
    -0.8717401485096066,
    -0.5917001814331423,
    -0.2092992179024789,
    0.2092992179024789,
    0.5917001814331423,
    0.8717401485096066,
    1.0,
)
GLL_WEIGHTS = (
    0.03571428571428571,
    0.21070422714350603,
    0.34112269248350435,
    0.4124587946587039,
    0.4124587946587039,
    0.34112269248350435,
    0.21070422714350603,
    0.03571428571428571,
)
SLOTS = 128
MESH = pl.DeviceIdType.MESH
F32 = jnp.float32
BF16 = jnp.bfloat16


def derivative_matrix():
    points = np.array(GLL_POINTS)
    identity = np.eye(8)
    spread = points[:, None] - points[None, :] + identity
    products = np.prod(spread, axis=1)
    matrix = products[:, None] / products[None, :] / spread
    off_diagonal = matrix * (1.0 - identity)
    return off_diagonal - identity * off_diagonal.sum(axis=1)[:, None]


DMAT = derivative_matrix()

ROW_POINT = 0
ROW_NORM = 8
ROW_ROLL = 16
ROW_WEIGHT = 80
ROW_RADIAL = 112


def constant_table():
    points = np.array(GLL_POINTS)
    weights = np.array(GLL_WEIGHTS)
    rows = [np.repeat(points[:, None], 128, axis=1)]
    spread = points[:, None] - points[None, :] + np.eye(8)
    rows.append(np.repeat((1.0 / np.prod(spread, axis=1))[:, None], 128, axis=1))
    for shift in range(8):
        coef = np.array([DMAT[i, (i - shift) % 8] for i in range(8)])
        rows.append(np.repeat(coef[:, None], 128, axis=1))
    rows.append(np.tile(weights, 4)[:, None] * np.tile(weights, 16)[None, :])
    rows.append(np.kron(np.eye(16), DMAT.T))
    return np.concatenate(rows, axis=0).astype(np.float32)


def quadrature_rows(length):
    steps = np.arange(length, dtype=np.float32)
    quad = np.sqrt(steps + np.float32(1.0)) - np.sqrt(steps)
    rows = np.zeros((16, length, 3), np.float32)
    for comp in range(3):
        rows[comp, :, comp] = quad
    return rows.reshape(16, length * 3)


def split3(values):
    high = values.astype(BF16).astype(F32)
    rest = values - high
    mid = rest.astype(BF16).astype(F32)
    return high, mid, rest - mid


def kernel(
    n_ax, n_xs,
    vel_ref, scale_ref, part_ref, elem_ref, ref_ref, bvel_ref, tau_ref, coef_ref,
    hist_ref, const_ref, quad_ref,
    fluid_ref, bubble_ref,
    hist_buf, lhs, onehot, sendq, recvq, sendr, recvr, table, wsum, weights_za,
    face_out, face_in, plane_out, plane_in,
    local_sem, q_send, q_recv, r_send, r_recv, h_send, h_recv,
):
    ax = lax.axis_index("ax")
    me = lax.axis_index("xs")
    held = part_ref.shape[1]

    barrier = pltpu.get_barrier_semaphore()

    def greet(step, carry):
        pl.semaphore_signal(
            barrier, inc=1, device_id=(ax, lax.rem(me + step, n_xs)), device_id_type=MESH
        )
        return carry

    lax.fori_loop(1, n_xs, greet, 0)
    up, down = lax.rem(ax + 1, n_ax), lax.rem(ax + n_ax - 1, n_ax)
    for other in (up, down):
        pl.semaphore_signal(barrier, inc=1, device_id=(other, me), device_id_type=MESH)

    load_hist = pltpu.make_async_copy(hist_ref, hist_buf, local_sem)
    load_hist.start()

    rel = part_ref[...] - me
    rel = jnp.where(rel < 0, rel + n_xs, rel)
    member = (
        jnp.broadcast_to(rel, (n_xs, held))
        == lax.broadcasted_iota(jnp.int32, (n_xs, held), 0)
    ).astype(F32)
    chunks = held // 128
    pieces = [member[:, c * 128 : (c + 1) * 128] for c in range(chunks)]
    stacked = jnp.concatenate(pieces, axis=0).astype(BF16)
    before = (
        lax.broadcasted_iota(jnp.int32, (128, 128), 0)
        < lax.broadcasted_iota(jnp.int32, (128, 128), 1)
    ).astype(F32).astype(BF16)
    counts = jnp.dot(stacked, before, preferred_element_type=F32)
    totals = jnp.dot(stacked, jnp.ones((128, 128), BF16), preferred_element_type=F32)
    carry = jnp.zeros((n_xs, 128), F32)
    ranks = []
    for c in range(chunks):
        rows = slice(c * n_xs, (c + 1) * n_xs)
        ranks.append(jnp.sum(pieces[c] * (counts[rows] + carry), axis=0, keepdims=True))
        carry = carry + totals[rows]
    rank = jnp.concatenate(ranks, axis=1).astype(jnp.int32)
    onehot[...] = (
        jnp.broadcast_to(rank, (SLOTS, held))
        == lax.broadcasted_iota(jnp.int32, (SLOTS, held), 0)
    ).astype(F32).astype(BF16)

    query = jnp.concatenate(
        [ref_ref[...], elem_ref[...].astype(F32), tau_ref[...], jnp.zeros((3, held), F32)],
        axis=0,
    )
    parts = split3(query)
    rel8 = jnp.broadcast_to(rel, (8, held))
    span = 8 * n_xs

    for which in range(3):
        for step in range(0, n_xs, 2):
            pair = jnp.concatenate(
                [jnp.where(rel8 == step + i, parts[which], 0.0) for i in range(2)], axis=0
            )
            lhs[which * span + 8 * step : which * span + 8 * step + 16, :] = pair.astype(BF16)
    slots = lax.dot_general(
        lhs[...], onehot[...], (((1,), (1,)), ((), ())), preferred_element_type=F32
    )
    slots = slots[:span] + slots[span : 2 * span] + slots[2 * span :]
    slots = slots.reshape(n_xs, 8, SLOTS)
    sendq[...] = slots
    recvq[0] = slots[0]

    pl.semaphore_wait(barrier, n_xs + 1)

    def query_copy(step, target):
        return pltpu.make_async_remote_copy(
            src_ref=sendq.at[step, pl.ds(0, 5)],
            dst_ref=recvq.at[step, pl.ds(0, 5)],
            send_sem=q_send.at[step],
            recv_sem=q_recv.at[step],
            device_id=(ax, target),
            device_id_type=MESH,
        )

    def send_query(step, carry):
        query_copy(step, lax.rem(me + step, n_xs)).start()
        return carry

    lax.fori_loop(1, n_xs, send_query, 0)

    vel = vel_ref[...]
    length_a, length_r = vel.shape[2], vel.shape[3]
    nodes = 8 * length_a
    grad_r = jnp.dot(
        vel.reshape(3 * nodes, length_r),
        const_ref[ROW_RADIAL : ROW_RADIAL + 128, :],
        preferred_element_type=F32,
        precision=lax.Precision.HIGHEST,
    ).reshape(vel.shape)
    scale = scale_ref[...]
    inverse = const_ref[ROW_WEIGHT : ROW_WEIGHT + 32, :] / (scale[0] * scale[1] * scale[2])
    lane = lax.broadcasted_iota(jnp.int32, (4, length_a, length_r), 2)
    upper = (lane % 8 == 7) & (lane < length_r - 1)
    lower = (lane % 8 == 0) & (lane > 0)
    for z in range(8):
        here = vel[:, z]
        grad_z = sum(float(DMAT[z, j]) * vel[:, j] for j in range(8) if abs(DMAT[z, j]) > 1e-9)
        groups = here.reshape(3 * length_a // 8, 8, length_r)
        grad_a = const_ref[ROW_ROLL : ROW_ROLL + 8, :] * groups
        for shift in range(1, 8):
            coef = const_ref[ROW_ROLL + 8 * shift : ROW_ROLL + 8 * shift + 8, :]
            grad_a = grad_a + coef * pltpu.roll(groups, shift, 1)
        grad_a = grad_a.reshape(here.shape)
        advect = (
            (here[0] * scale[0])[None] * grad_z
            + (here[1] * scale[1])[None] * grad_a
            + (here[2] * scale[2])[None] * grad_r[:, z]
        )
        for comp in range(3):
            row = comp * nodes + z * length_a
            table[row : row + length_a, :] = here[comp].astype(BF16)
            row = row + 3 * nodes
            table[row : row + length_a, :] = advect[comp].astype(BF16)
        mass = GLL_WEIGHTS[z] * inverse
        weighted = jnp.concatenate([mass[None] * advect, mass[None]], axis=0)
        after = pltpu.roll(weighted, length_r - 1, 2)
        prior = pltpu.roll(weighted, 1, 2)
        wsum[:, z] = weighted + jnp.where(upper, after, jnp.where(lower, prior, 0.0))

    for edge in range(8, length_a, 8):
        both = wsum[:, :, edge - 1 : edge, :] + wsum[:, :, edge : edge + 1, :]
        wsum[:, :, edge - 1 : edge, :] = both
        wsum[:, :, edge : edge + 1, :] = both
    for z in range(8):
        face_out[0, :, z : z + 1, :] = wsum[:, z, length_a - 1 : length_a, :]
        face_out[1, :, z : z + 1, :] = wsum[:, z, 0:1, :]

    def face_copy(side):
        target = lax.rem(me + (1 if side == 0 else n_xs - 1), n_xs)
        return pltpu.make_async_remote_copy(
            src_ref=face_out.at[side],
            dst_ref=face_in.at[side],
            send_sem=h_send.at[side],
            recv_sem=h_recv.at[side],
            device_id=(ax, target),
            device_id_type=MESH,
        )

    def plane_copy(side):
        return pltpu.make_async_remote_copy(
            src_ref=plane_out.at[side],
            dst_ref=plane_in.at[side],
            send_sem=h_send.at[2 + side],
            recv_sem=h_recv.at[2 + side],
            device_id=(up if side == 0 else down, me),
            device_id_type=MESH,
        )

    faces = [face_copy(side) for side in range(2)]
    for face in faces:
        face.start()

    load_hist.wait()
    basset = jnp.dot(quad_ref[...], hist_buf[...], preferred_element_type=F32)[0:3]
    local = coef_ref[...] * basset - tau_ref[...] * bvel_ref[...]

    faces[0].wait()
    faces[1].wait()
    for z in range(8):
        wsum[:, z, 0:1, :] = wsum[:, z, 0:1, :] + face_in[0, :, z : z + 1, :]
        last = slice(length_a - 1, length_a)
        wsum[:, z, last, :] = wsum[:, z, last, :] + face_in[1, :, z : z + 1, :]
    plane_out[0] = wsum[:, 7]
    plane_out[1] = wsum[:, 0]
    planes = [plane_copy(side) for side in range(2)]
    for plane in planes:
        plane.start()

    def answer_copy(step):
        return pltpu.make_async_remote_copy(
            src_ref=sendr.at[step, pl.ds(0, 3)],
            dst_ref=recvr.at[step, pl.ds(0, 3)],
            send_sem=r_send.at[step],
            recv_sem=r_recv.at[step],
            device_id=(ax, lax.rem(me + n_xs - step, n_xs)),
            device_id_type=MESH,
        )

    point = jnp.concatenate([const_ref[ROW_POINT : ROW_POINT + 8, :]] * 2, axis=1)
    norm = jnp.concatenate([const_ref[ROW_NORM : ROW_NORM + 8, :]] * 2, axis=1)

    def lagrange(row):
        diff = row - point
        one = pltpu.roll(diff, 1, 0)
        two = one * pltpu.roll(one, 1, 0)
        four = two * pltpu.roll(two, 2, 0)
        rest = four * pltpu.roll(two, 4, 0) * pltpu.roll(one, 6, 0)
        return (rest * norm).astype(BF16).astype(F32)

    def serve(pair, carry):
        first_step = 2 * pair

        @pl.when(pair > 0)
        def _():
            query_copy(first_step, me).wait_recv()

        query_copy(first_step + 1, me).wait_recv()
        both = jnp.concatenate([recvq[first_step], recvq[first_step + 1]], axis=1)
        lag_z = lagrange(both[0:1])
        lag_a = lagrange(both[1:2])
        lag_r = lagrange(both[2:3])
        element = both[3:4].astype(jnp.int32)
        radial = jnp.broadcast_to(element & 15, (8, 2 * SLOTS))
        azimuth = jnp.broadcast_to((element >> 4) & 3, (8, 2 * SLOTS))
        tau = both[4:5]
        weight_r = jnp.concatenate(
            [jnp.where(radial == e, lag_r, 0.0) for e in range(length_r // 8)], axis=0
        ).astype(BF16)
        masked = jnp.concatenate(
            [jnp.where(azimuth == e, lag_a, 0.0) for e in range(length_a // 8)], axis=0
        )
        for z in range(8):
            weights_za[z * length_a : (z + 1) * length_a, :] = lag_z[z : z + 1] * masked
        sums = []
        for field in range(6):
            first = jnp.dot(
                table[field * nodes : (field + 1) * nodes, :],
                weight_r,
                preferred_element_type=F32,
            )
            product = (first * weights_za[...]).reshape(nodes // 8, 8, 2 * SLOTS)
            sums.append(jnp.sum(product, axis=0))
        for comp in range(3):
            value = jnp.sum(3.0 * sums[3 + comp] + tau * sums[comp], axis=0, keepdims=True)
            sendr[first_step, comp : comp + 1, :] = value[:, :SLOTS]
            sendr[first_step + 1, comp : comp + 1, :] = value[:, SLOTS:]

        @pl.when(pair > 0)
        def _():
            answer_copy(first_step).start()

        answer_copy(first_step + 1).start()
        return carry

    lax.fori_loop(0, n_xs // 2, serve, 0)

    planes[0].wait()
    planes[1].wait()
    for z in range(8):
        total = wsum[:, z]
        if z == 0:
            total = total + plane_in[0]
        if z == 7:
            total = total + plane_in[1]
        fluid_ref[:, z] = total[0:3] * (-1.0 / total[3:4])

    recvr[0, 0:3] = sendr[0, 0:3]

    def finish(step, carry):
        query_copy(step, me).wait_send()
        answer_copy(step).wait()
        return carry

    lax.fori_loop(1, n_xs, finish, 0)

    answers = recvr[...].reshape(span, SLOTS)
    spread = jnp.dot(
        jnp.concatenate([p.astype(BF16) for p in split3(answers)], axis=0),
        onehot[...],
        preferred_element_type=F32,
    )
    total = jnp.zeros((8, held), F32)
    for step in range(n_xs):
        rows = [spread[w * span + 8 * step : w * span + 8 * step + 8] for w in range(3)]
        total = total + jnp.where(rel8 == step, rows[0] + rows[1] + rows[2], 0.0)
    bubble_ref[...] = total[0:3] + local


def shards(
    velocity, metric, bubble_part, bubble_elem, bubble_ref, bubble_vel, inv_tau,
    basset_coef, history,
):
    n_ax, n_xs = lax.axis_size("ax"), lax.axis_size("xs")
    held = bubble_part.shape[0]
    steps = history.shape[0]
    _, length_z, length_a, length_r = velocity.shape
    scale = jnp.repeat(jnp.repeat(metric[:, 0], 8, axis=1), 8, axis=2)
    const = jnp.asarray(constant_table())
    quad = jnp.asarray(quadrature_rows(steps), BF16)
    nodes = length_z * length_a
    vmem = pl.BlockSpec(memory_space=pltpu.VMEM)
    anywhere = pl.BlockSpec(memory_space=pl.ANY)
    dma = pltpu.SemaphoreType.DMA
    return pl.pallas_call(
        functools.partial(kernel, n_ax, n_xs),
        out_shape=(
            jax.ShapeDtypeStruct(velocity.shape, F32),
            jax.ShapeDtypeStruct((3, held), F32),
        ),
        in_specs=[vmem] * 8 + [anywhere] + [vmem] * 2,
        out_specs=(vmem, vmem),
        scratch_shapes=[
            pltpu.VMEM((3 * steps, held), BF16),
            pltpu.VMEM((3 * 8 * n_xs, held), BF16),
            pltpu.VMEM((SLOTS, held), BF16),
            pltpu.VMEM((n_xs, 8, SLOTS), F32),
            pltpu.VMEM((n_xs, 8, SLOTS), F32),
            pltpu.VMEM((n_xs, 8, SLOTS), F32),
            pltpu.VMEM((n_xs, 8, SLOTS), F32),
            pltpu.VMEM((6 * nodes, length_r), BF16),
            pltpu.VMEM((4, length_z, length_a, length_r), F32),
            pltpu.VMEM((nodes, 2 * SLOTS), F32),
            pltpu.VMEM((2, 4, length_z, length_r), F32),
            pltpu.VMEM((2, 4, length_z, length_r), F32),
            pltpu.VMEM((2, 4, length_a, length_r), F32),
            pltpu.VMEM((2, 4, length_a, length_r), F32),
            dma,
            dma((n_xs,)),
            dma((n_xs,)),
            dma((n_xs,)),
            dma((n_xs,)),
            dma((4,)),
            dma((4,)),
        ],
        compiler_params=pltpu.CompilerParams(
            collective_id=0, has_side_effects=True, vmem_limit_bytes=40 * 1024 * 1024
        ),
    )(
        velocity,
        scale,
        bubble_part.reshape(1, held),
        bubble_elem.reshape(1, held),
        bubble_ref,
        bubble_vel,
        inv_tau.reshape(1, held),
        basset_coef.reshape(1, held),
        history.reshape(3 * steps, held),
        const,
        quad,
    )


def solution(mesh):
    return jax.shard_map(
        shards,
        mesh=mesh,
        in_specs=(
            P(None, "ax", "xs", None),
            P(None, "ax", "xs", None),
            P(("ax", "xs")),
            P(("ax", "xs")),
            P(None, ("ax", "xs")),
            P(None, ("ax", "xs")),
            P(("ax", "xs")),
            P(("ax", "xs")),
            P(None, None, ("ax", "xs")),
        ),
        out_specs=(P(None, "ax", "xs", None), P(None, ("ax", "xs"))),
        check_vma=False,
    )
```

time: 239 us -> 35.4 us (0.15)
  local copies, waits for them, and re-layouts: 126 us -> 4.86 us
  other arithmetic: 63.5 us -> 0 us
  starting transfers between devices: 35.5 us -> 0 us
  Pallas kernels: 0 us -> 29.6 us
  matrix products: 4.88 us -> 0 us
  waiting for transfers between devices: 4.7 us -> 0 us
    gather x26 -> x0, local copies, waits for them, and re-layouts: 82.9 us -> none  [the longest x24 76 us: interpolate(): jnp.take(table, element.reshape(-1), axis=0)]
    while x160 -> x0, other arithmetic: 36.6 us -> none
    pallas_call x0 -> x1, Pallas kernels: none -> 29.6 us  [shards(): pl.pallas_call(functools.partial(kernel, n_ax, n_xs), out_shape=(jax.Shap...]
    ppermute x4 -> x0, starting transfers between devices: 18.5 us -> none  [the longest x2 12 us: with_halo(): lax.ppermute(head, axis, [((i + 1) % count, i) for i in range(count)])]
    all_to_all x2 -> x0, starting transfers between devices: 17 us -> none  [the longest x1 9.2 us: shards(): lax.all_to_all(outgoing, 'xs', split_axis=0, concat_axis=0, tiled=True)]
    another operation x27 -> x0, other arithmetic: 9.57 us -> none
    concatenate x2 -> x0, local copies, waits for them, and re-layouts: 8.22 us -> none  [shards(): source = jnp.concatenate([velocity, advect], axis=0).astype(jnp.bfloat16)]
    transpose x3 -> x0, local copies, waits for them, and re-layouts: 6.98 us -> none  [the longest x1 6.52 us: element_table(): return blocks.transpose(1, 3, 5, 0, 2, 4, 6).reshape(-1, fields * 512)]
  transfers between devices with their start and end apart: 6 -> 0, of which waited for: 1 -> 0; matrix products, arithmetic and copies ran while one was open for 74% -> 0% of each run, Pallas kernels for 0% -> 0%
where the time goes in v1:
time: 35.4 us; the launch traced here: 35.3 us
  Pallas kernels  29.6 us (84%)
  local copies, waits for them, and re-layouts  4.86 us (14%)
  between operations  0.77 us (2%)
    pallas_call x1, Pallas kernels, shards(): pl.pallas_call(functools.partial(kernel, n_ax, n_xs), out_shape=(jax.Shap...  29.6 us
    unnamed x23, local copies, waits for them, and re-layouts  3.97 us

profile of v1, /device:TPU:1, one launch (start us, length us, event | category | flops | bytes accessed | tf_op | source)
XLA Modules:
  0.0 35.3 jit_solution(9224867833351258709)
XLA Ops:
  0.6 0.0 copy-start
  0.6 1.8 %copy.18 = bf16[128,3,1024]{2,1,0:T(4,128)(2,1)S(1)} copy(bf16[128,3,1024]{2,0,1:T(8,128)(2,1)} %param.19) | data formatting | bytes 1572864 | tf_op args[8]
  2.5 0.7 %reshape.31.hist_ref = bf16[384,1024]{1,0:T(8,128)(2,1)S(1)} reshape(bf16[128,3,1024]{2,1,0:T(4,128)(2,1)S(1)} %copy.18) | data formatting | bytes 1572864 | tf_op jit(solution)/shard_map/reshape | solution.py:428
  3.2 0.0 copy-done
  3.2 0.0 copy-start.1
  3.2 0.1 copy.17
  3.3 0.0 copy-start.2
  3.3 0.0 copy-start.3
  3.3 0.0 copy-start.4
  3.3 0.0 copy-start.5
  3.3 0.0 copy-start.7
  3.4 0.0 copy-start.8
  3.4 0.0 copy-start.9
  3.4 0.1 copy.19.scale_ref
  3.5 0.0 copy-start.6
  3.5 0.7 %copy-done.1 = f32[3,8,32,128]{3,2,1,0:T(8,128)S(1)} copy-done((f32[3,8,32,128]{3,2,1,0:T(8,128)S(1)}, f32[3,8,32,128]{3,2,1,0:T(8,128)}, u32[]{:S(2)}) %copy-start.1) | copy-done | bytes 393240
  4.2 0.1 copy-done.2
  4.2 0.0 copy-done.3
  4.2 0.0 copy-done.4
  4.2 0.0 copy-done.5
  4.2 0.0 copy-done.7
  4.2 0.0 copy-done.8
  4.3 0.0 copy-done.9
  4.3 0.0 copy-done.6
  4.3 29.6 %shard_map.122 = (f32[3,8,32,128]{3,2,1,0:T(8,128)S(1)}, f32[3,1024]{1,0:T(4,128)S(1)}) custom-call(f32[3,8,32,128]{3,2,1,0:T(8,128)S(1)} %copy-done.1, f32[3,32,128]{2,1,0:T(8,128)S(1)} %copy.19.scale_ref, s32[1,1024]{1,0:T(1,128)S(1)} %bitcast.10, s32[1,1024]{1,0:T(1,128)S(1)} %bitcast.11, f32[3,1024]{1,0:T(4,128)S(1)} %copy-done.3, ...), custom_call_target="tpu_custom_call" | custom-call | tf_op jit(solution)/shard_map/pallas_call | solution.py:385
  33.9 0.7 %copy.22 = f32[3,8,32,128]{3,2,1,0:T(8,128)} copy(f32[3,8,32,128]{3,2,1,0:T(8,128)S(1)} %get-tuple-element.4) | data formatting | bytes 786432
  34.7 0.6 %copy.23 = f32[3,1024]{1,0:T(4,128)} copy(f32[3,1024]{1,0:T(4,128)S(1)} %get-tuple-element.5) | data formatting | bytes 24576
  (2 shorter events, 0.0 us)
Async XLA Ops:
  0.6 2.5 %copy-start = (f32[3,1,4,16]{3,2,1,0:T(4,128)S(1)}, f32[3,1,4,16]{3,2,1,0:T(4,128)}, u32[]{:S(2)}) copy-start(f32[3,1,4,16]{3,2,1,0:T(4,128)} %param.12) | copy-start | bytes 2308
  3.2 1.0 %copy-start.1 = (f32[3,8,32,128]{3,2,1,0:T(8,128)S(1)}, f32[3,8,32,128]{3,2,1,0:T(8,128)}, u32[]{:S(2)}) copy-start(f32[3,8,32,128]{3,2,1,0:T(8,128)} %vel_ref.1) | copy-start | bytes 1179652
  3.3 0.9 %copy-start.2 = (f32[240,128]{1,0:T(8,128)S(1)}, f32[240,128]{1,0:T(8,128)}, u32[]{:S(2)}) copy-start(f32[240,128]{1,0:T(8,128)} %constant.4.clone.const_ref) | copy-start | bytes 368644
  3.3 0.9 %copy-start.3 = (f32[3,1024]{1,0:T(4,128)S(1)}, f32[3,1024]{1,0:T(4,128)}, u32[]{:S(2)}) copy-start(f32[3,1024]{1,0:T(4,128)} %ref_ref.1) | copy-start | bytes 36868
  3.3 0.9 %copy-start.4 = (f32[3,1024]{1,0:T(4,128)S(1)}, f32[3,1024]{1,0:T(4,128)}, u32[]{:S(2)}) copy-start(f32[3,1024]{1,0:T(4,128)} %bvel_ref.1) | copy-start | bytes 36868
  3.3 0.9 %copy-start.5 = (bf16[16,384]{1,0:T(8,128)(2,1)S(1)}, bf16[16,384]{1,0:T(8,128)(2,1)}, u32[]{:S(2)}) copy-start(bf16[16,384]{1,0:T(8,128)(2,1)} %constant.5.clone.quad_ref) | copy-start | bytes 36868
  3.3 0.9 %copy-start.7 = (s32[1024]{0:T(1024)S(1)}, s32[1024]{0:T(1024)}, u32[]{:S(2)}) copy-start(s32[1024]{0:T(1024)} %param.14) | copy-start | bytes 12292
  3.4 0.9 %copy-start.8 = (f32[1024]{0:T(1024)S(1)}, f32[1024]{0:T(1024)}, u32[]{:S(2)}) copy-start(f32[1024]{0:T(1024)} %param.17) | copy-start | bytes 12292
  3.4 0.9 %copy-start.9 = (f32[1024]{0:T(1024)S(1)}, f32[1024]{0:T(1024)}, u32[]{:S(2)}) copy-start(f32[1024]{0:T(1024)} %param.18) | copy-start | bytes 12292
  3.5 0.8 %copy-start.6 = (s32[1024]{0:T(1024)S(1)}, s32[1024]{0:T(1024)}, u32[]{:S(2)}) copy-start(s32[1024]{0:T(1024)} %param.13) | copy-start | bytes 12292

commit v2 on v1

v2 whole, which is shorter than its diff:
```python
import functools

import jax
import jax.numpy as jnp
import numpy as np
from jax import lax
from jax.experimental import pallas as pl
from jax.experimental.pallas import tpu as pltpu
from jax.sharding import PartitionSpec as P

GLL_POINTS = (
    -1.0,
    -0.8717401485096066,
    -0.5917001814331423,
    -0.2092992179024789,
    0.2092992179024789,
    0.5917001814331423,
    0.8717401485096066,
    1.0,
)
GLL_WEIGHTS = (
    0.03571428571428571,
    0.21070422714350603,
    0.34112269248350435,
    0.4124587946587039,
    0.4124587946587039,
    0.34112269248350435,
    0.21070422714350603,
    0.03571428571428571,
)
SLOTS = 128
GROUP = 4
MESH = pl.DeviceIdType.MESH
F32 = jnp.float32
BF16 = jnp.bfloat16


def derivative_matrix():
    points = np.array(GLL_POINTS)
    identity = np.eye(8)
    spread = points[:, None] - points[None, :] + identity
    products = np.prod(spread, axis=1)
    matrix = products[:, None] / products[None, :] / spread
    off_diagonal = matrix * (1.0 - identity)
    return off_diagonal - identity * off_diagonal.sum(axis=1)[:, None]


DMAT = derivative_matrix()

ROW_POINT = 0
ROW_NORM = 8
ROW_ROLL = 16
ROW_WEIGHT = 80
ROW_RADIAL = 112


def constant_table():
    points = np.array(GLL_POINTS)
    weights = np.array(GLL_WEIGHTS)
    rows = [np.repeat(points[:, None], 128, axis=1)]
    spread = points[:, None] - points[None, :] + np.eye(8)
    rows.append(np.repeat((1.0 / np.prod(spread, axis=1))[:, None], 128, axis=1))
    for shift in range(8):
        coef = np.array([DMAT[i, (i - shift) % 8] for i in range(8)])
        rows.append(np.repeat(coef[:, None], 128, axis=1))
    rows.append(np.tile(weights, 4)[:, None] * np.tile(weights, 16)[None, :])
    rows.append(np.kron(np.eye(16), DMAT.T))
    return np.concatenate(rows, axis=0).astype(np.float32)


def quadrature_rows(length):
    steps = np.arange(length, dtype=np.float32)
    quad = np.sqrt(steps + np.float32(1.0)) - np.sqrt(steps)
    rows = np.zeros((16, 3, length), np.float32)
    for comp in range(3):
        rows[comp, comp] = quad
    return rows.reshape(16, 3 * length)


def split3(values):
    high = values.astype(BF16).astype(F32)
    rest = values - high
    mid = rest.astype(BF16).astype(F32)
    return high, mid, rest - mid


def ranked(rel, n_xs, onehot):
    held = rel.shape[1]
    member = (
        jnp.broadcast_to(rel, (n_xs, held))
        == lax.broadcasted_iota(jnp.int32, (n_xs, held), 0)
    ).astype(F32)
    chunks = held // 128
    pieces = [member[:, c * 128 : (c + 1) * 128] for c in range(chunks)]
    stacked = jnp.concatenate(pieces, axis=0).astype(BF16)
    before = (
        lax.broadcasted_iota(jnp.int32, (128, 128), 0)
        < lax.broadcasted_iota(jnp.int32, (128, 128), 1)
    ).astype(F32).astype(BF16)
    counts = jnp.dot(stacked, before, preferred_element_type=F32)
    totals = jnp.dot(stacked, jnp.ones((128, 128), BF16), preferred_element_type=F32)
    carry = jnp.zeros((n_xs, 128), F32)
    ranks = []
    for c in range(chunks):
        rows = slice(c * n_xs, (c + 1) * n_xs)
        ranks.append(jnp.sum(pieces[c] * (counts[rows] + carry), axis=0, keepdims=True))
        carry = carry + totals[rows]
    rank = jnp.concatenate(ranks, axis=1).astype(jnp.int32)
    onehot[...] = (
        jnp.broadcast_to(rank, (SLOTS, held))
        == lax.broadcasted_iota(jnp.int32, (SLOTS, held), 0)
    ).astype(F32).astype(BF16)


def dispatch(rel, n_xs, coords, elem, lhs, onehot, sendq, recvq):
    held = rel.shape[1]
    high, mid, low = split3(coords)
    packed = jnp.concatenate(
        [high, elem, jnp.zeros((3, held), F32), mid, low], axis=0
    ).astype(BF16)
    rel16 = jnp.broadcast_to(rel, (16, held))
    zero = jnp.zeros((16, held), BF16)
    for step in range(n_xs):
        lhs[16 * step : 16 * step + 16, :] = jnp.where(rel16 == step, packed, zero)
    slots = lax.dot_general(
        lhs[...], onehot[...], (((1,), (1,)), ((), ())), preferred_element_type=F32
    ).reshape(n_xs, 2, 8, SLOTS)
    rest = slots[:, 1]
    rest = rest + pltpu.roll(rest, 4, 1)
    row = lax.broadcasted_iota(jnp.int32, (n_xs, 8, SLOTS), 1)
    slots = slots[:, 0] + jnp.where(row < 4, rest, 0.0)
    sendq[...] = slots
    recvq[0] = slots[0]


def advection(vel_ref, scale_ref, const_ref, table, wsum):
    vel = vel_ref[...]
    length_a, length_r = vel.shape[2], vel.shape[3]
    nodes = 8 * length_a
    grad_r = jnp.dot(
        vel.reshape(3 * nodes, length_r),
        const_ref[ROW_RADIAL : ROW_RADIAL + 128, :],
        preferred_element_type=F32,
        precision=lax.Precision.HIGHEST,
    ).reshape(vel.shape)
    scale = scale_ref[...]
    inverse = const_ref[ROW_WEIGHT : ROW_WEIGHT + 32, :] / (scale[0] * scale[1] * scale[2])
    lane = lax.broadcasted_iota(jnp.int32, (4, length_a, length_r), 2)
    upper = (lane % 8 == 7) & (lane < length_r - 1)
    lower = (lane % 8 == 0) & (lane > 0)
    for z in range(8):
        here = vel[:, z]
        grad_z = sum(float(DMAT[z, j]) * vel[:, j] for j in range(8) if abs(DMAT[z, j]) > 1e-9)
        groups = here.reshape(3 * length_a // 8, 8, length_r)
        grad_a = const_ref[ROW_ROLL : ROW_ROLL + 8, :] * groups
        for shift in range(1, 8):
            coef = const_ref[ROW_ROLL + 8 * shift : ROW_ROLL + 8 * shift + 8, :]
            grad_a = grad_a + coef * pltpu.roll(groups, shift, 1)
        grad_a = grad_a.reshape(here.shape)
        advect = (
            (here[0] * scale[0])[None] * grad_z
            + (here[1] * scale[1])[None] * grad_a
            + (here[2] * scale[2])[None] * grad_r[:, z]
        )
        fields = [here[0], here[1], here[2], advect[0], advect[1], advect[2]]
        if z % 2 == 1:
            for field in range(6):
                for element in range(length_a // 8):
                    rows = slice(8 * element, 8 * element + 8)
                    pair = jnp.concatenate([earlier[field][rows], fields[field][rows]], axis=0)
                    table[
                        64 * field + 8 * (z - 1) : 64 * field + 8 * (z + 1),
                        length_r * element : length_r * (element + 1),
                    ] = pair.astype(BF16)
        earlier = fields
        mass = GLL_WEIGHTS[z] * inverse
        weighted = jnp.concatenate([mass[None] * advect, mass[None]], axis=0)
        after = pltpu.roll(weighted, length_r - 1, 2)
        prior = pltpu.roll(weighted, 1, 2)
        wsum[:, z] = weighted + jnp.where(upper, after, jnp.where(lower, prior, 0.0))


def azimuth_pairs(wsum, face_out):
    length_a = wsum.shape[2]
    for edge in range(8, length_a, 8):
        both = wsum[:, :, edge - 1 : edge, :] + wsum[:, :, edge : edge + 1, :]
        wsum[:, :, edge - 1 : edge, :] = both
        wsum[:, :, edge : edge + 1, :] = both
    for z in range(8):
        face_out[0, :, z : z + 1, :] = wsum[:, z, length_a - 1 : length_a, :]
        face_out[1, :, z : z + 1, :] = wsum[:, z, 0:1, :]


def add_faces(wsum, face_in, plane_out):
    length_a = wsum.shape[2]
    last = slice(length_a - 1, length_a)
    for z in range(8):
        wsum[:, z, 0:1, :] = wsum[:, z, 0:1, :] + face_in[0, :, z : z + 1, :]
        wsum[:, z, last, :] = wsum[:, z, last, :] + face_in[1, :, z : z + 1, :]
    plane_out[0] = wsum[:, 7]
    plane_out[1] = wsum[:, 0]


def fluid_finish(wsum, plane_in, fluid_ref):
    for z in range(8):
        total = wsum[:, z]
        if z == 0:
            total = total + plane_in[0]
        if z == 7:
            total = total + plane_in[1]
        fluid_ref[:, z] = total[0:3] * (-1.0 / total[3:4])


def interpolate(both, const_ref, table):
    width = both.shape[1]
    point = jnp.concatenate([const_ref[ROW_POINT : ROW_POINT + 8, :]] * (width // 128), axis=1)
    norm = jnp.concatenate([const_ref[ROW_NORM : ROW_NORM + 8, :]] * (width // 128), axis=1)

    def lagrange(row):
        diff = row - point
        one = pltpu.roll(diff, 1, 0)
        two = one * pltpu.roll(one, 1, 0)
        four = two * pltpu.roll(two, 2, 0)
        rest = four * pltpu.roll(two, 4, 0) * pltpu.roll(one, 6, 0)
        return (rest * norm).astype(BF16).astype(F32)

    lag_z = lagrange(both[0:1])
    lag_a = lagrange(both[1:2])
    lag_r = lagrange(both[2:3])
    tau = both[3:4]
    element = both[4:5].astype(jnp.int32)
    radial = jnp.broadcast_to(element & 15, (8, width))
    azimuth = jnp.broadcast_to((element >> 4) & 3, (128, width))
    weight_r = jnp.concatenate(
        [jnp.where(radial == e, lag_r, 0.0) for e in range(16)], axis=0
    ).astype(BF16)
    zero = jnp.zeros_like(weight_r)
    weight = jnp.concatenate(
        [jnp.where(azimuth == e, weight_r, zero) for e in range(4)], axis=0
    )
    first = jnp.dot(table[...], weight, preferred_element_type=F32)
    sums = []
    for field in range(6):
        total = jnp.zeros((8, width), F32)
        for z in range(8):
            row = 64 * field + 8 * z
            total = total + first[row : row + 8] * lag_z[z : z + 1]
        sums.append(total * lag_a)
    return [
        jnp.sum(3.0 * sums[3 + comp] + tau * sums[comp], axis=0, keepdims=True)
        for comp in range(3)
    ]


def gather(rel8, n_xs, recvr, onehot):
    held = rel8.shape[1]
    answers = recvr[...].reshape(4 * n_xs, SLOTS)
    spread = jnp.dot(
        jnp.concatenate([p.astype(BF16) for p in split3(answers)], axis=0),
        onehot[...],
        preferred_element_type=F32,
    )
    span = 4 * n_xs
    half = lax.broadcasted_iota(jnp.int32, (8, held), 0) // 4
    total = jnp.zeros((8, held), F32)
    for pair in range(n_xs // 2):
        rows = [spread[w * span + 8 * pair : w * span + 8 * pair + 8] for w in range(3)]
        total = total + jnp.where(rel8 - half == 2 * pair, rows[0] + rows[1] + rows[2], 0.0)
    total = total + pltpu.roll(total, 4, 0)
    return total[0:3]


def kernel(
    n_ax, n_xs,
    part_ref, elem_ref, ref_ref, bvel_ref, tau_ref, coef_ref, scale_ref, const_ref, quad_ref,
    vel_hbm, hist_hbm,
    fluid_ref, bubble_ref,
    vel_ref, hist_ref, lhs, onehot, sendq, recvq, sendr, recvr, table, wsum,
    face_out, face_in, plane_out, plane_in,
    local_sem, q_send, q_recv, r_send, r_recv, h_send, h_recv,
):
    ax = lax.axis_index("ax")
    me = lax.axis_index("xs")
    held = part_ref.shape[1]
    up, down = lax.rem(ax + 1, n_ax), lax.rem(ax + n_ax - 1, n_ax)

    load_vel = pltpu.make_async_copy(vel_hbm, vel_ref, local_sem.at[0])
    load_vel.start()
    load_hist = pltpu.make_async_copy(hist_hbm, hist_ref, local_sem.at[1])
    load_hist.start()

    def wrap(place):
        return jnp.where(place >= n_xs, place - n_xs, place)

    barrier = pltpu.get_barrier_semaphore()
    for step in range(1, n_xs):
        pl.semaphore_signal(
            barrier, inc=1, device_id=(ax, wrap(me + step)), device_id_type=MESH
        )
    for other in (up, down):
        pl.semaphore_signal(barrier, inc=1, device_id=(other, me), device_id_type=MESH)

    def query_copy(first, count, group, target):
        return pltpu.make_async_remote_copy(
            src_ref=sendq.at[pl.ds(first, count), pl.ds(0, 5)],
            dst_ref=recvq.at[pl.ds(first, count), pl.ds(0, 5)],
            send_sem=q_send,
            recv_sem=q_recv.at[group],
            device_id=(ax, target),
            device_id_type=MESH,
        )

    def answer_copy(tile, count, odd, step):
        return pltpu.make_async_remote_copy(
            src_ref=sendr.at[pl.ds(tile, count), pl.ds(4 * odd, 3)],
            dst_ref=recvr.at[pl.ds(tile, count), pl.ds(4 * odd, 3)],
            send_sem=r_send.at[odd],
            recv_sem=r_recv.at[odd],
            device_id=(ax, wrap(me + n_xs - step)),
            device_id_type=MESH,
        )

    def face_copy(side):
        return pltpu.make_async_remote_copy(
            src_ref=face_out.at[side],
            dst_ref=face_in.at[side],
            send_sem=h_send.at[side],
            recv_sem=h_recv.at[side],
            device_id=(ax, wrap(me + (1 if side == 0 else n_xs - 1))),
            device_id_type=MESH,
        )

    def plane_copy(side):
        return pltpu.make_async_remote_copy(
            src_ref=plane_out.at[side],
            dst_ref=plane_in.at[side],
            send_sem=h_send.at[2 + side],
            recv_sem=h_recv.at[2 + side],
            device_id=(up if side == 0 else down, me),
            device_id_type=MESH,
        )

    rel = part_ref[...] - me
    rel = jnp.where(rel < 0, rel + n_xs, rel)
    ranked(rel, n_xs, onehot)
    coords = jnp.concatenate([ref_ref[...], tau_ref[...]], axis=0)
    dispatch(rel, n_xs, coords, elem_ref[...].astype(F32), lhs, onehot, sendq, recvq)
    pl.semaphore_wait(barrier, n_xs + 1)
    for step in range(1, n_xs):
        query_copy(step, 1, (step - 1) // GROUP, wrap(me + step)).start()

    load_vel.wait()
    advection(vel_ref, scale_ref, const_ref, table, wsum)
    azimuth_pairs(wsum, face_out)
    for side in range(2):
        face_copy(side).start()

    def serve(group, count):
        first = GROUP * group + 1
        query_copy(first, count, group, me).wait_recv()
        sources = [recvq[first + i] for i in range(count)]
        if count < GROUP:
            sources.append(recvq[0])
        values = interpolate(jnp.concatenate(sources, axis=1), const_ref, table)
        for i in range(GROUP):
            lanes = slice(SLOTS * i, SLOTS * (i + 1))
            if i == count:
                for comp in range(3):
                    recvr[0, comp : comp + 1, :] = values[comp][:, lanes]
            else:
                tile, odd = (GROUP // 2) * group + (1 + i) // 2, (1 + i) % 2
                for comp in range(3):
                    row = 4 * odd + comp
                    sendr[tile, row : row + 1, :] = values[comp][:, lanes]
                answer_copy(tile, 1, odd, first + i).start()

    groups = n_xs // GROUP

    def serve_step(group, carry):
        serve(group, GROUP)
        return carry

    lax.fori_loop(0, groups - 1, serve_step, 0)
    serve(groups - 1, GROUP - 1)

    for side in range(2):
        face_copy(side).wait()
    add_faces(wsum, face_in, plane_out)
    for side in range(2):
        plane_copy(side).start()

    load_hist.wait()
    basset = jnp.dot(quad_ref[...], hist_ref[...], preferred_element_type=F32)[0:3]
    local = coef_ref[...] * basset - tau_ref[...] * bvel_ref[...]

    for side in range(2):
        plane_copy(side).wait()
    fluid_finish(wsum, plane_in, fluid_ref)

    query_copy(1, n_xs - 1, 0, me).wait_send()
    answer_copy(1, n_xs // 2 - 1, 0, 0).wait()
    answer_copy(0, n_xs // 2, 1, 0).wait()
    rel8 = jnp.broadcast_to(rel, (8, held))
    bubble_ref[...] = gather(rel8, n_xs, recvr, onehot) + local


def shards(
    velocity, metric, bubble_part, bubble_elem, bubble_ref, bubble_vel, inv_tau,
    basset_coef, history,
):
    n_ax, n_xs = lax.axis_size("ax"), lax.axis_size("xs")
    held = bubble_part.shape[0]
    steps = history.shape[0]
    _, length_z, length_a, length_r = velocity.shape
    scale = jnp.repeat(jnp.repeat(metric[:, 0], 8, axis=1), 8, axis=2)
    const = jnp.asarray(constant_table())
    quad = jnp.asarray(quadrature_rows(steps), BF16)
    vmem = pl.BlockSpec(memory_space=pltpu.VMEM)
    anywhere = pl.BlockSpec(memory_space=pl.ANY)
    dma = pltpu.SemaphoreType.DMA
    return pl.pallas_call(
        functools.partial(kernel, n_ax, n_xs),
        out_shape=(
            jax.ShapeDtypeStruct(velocity.shape, F32),
            jax.ShapeDtypeStruct((3, held), F32),
        ),
        in_specs=[vmem] * 9 + [anywhere] * 2,
        out_specs=(vmem, vmem),
        scratch_shapes=[
            pltpu.VMEM(velocity.shape, F32),
            pltpu.VMEM((3 * steps, held), BF16),
            pltpu.VMEM((16 * n_xs, held), BF16),
            pltpu.VMEM((SLOTS, held), BF16),
            pltpu.VMEM((n_xs, 8, SLOTS), F32),
            pltpu.VMEM((n_xs, 8, SLOTS), F32),
            pltpu.VMEM((n_xs // 2, 8, SLOTS), F32),
            pltpu.VMEM((n_xs // 2, 8, SLOTS), F32),
            pltpu.VMEM((6 * 64, 4 * length_r), BF16),
            pltpu.VMEM((4, length_z, length_a, length_r), F32),
            pltpu.VMEM((2, 4, length_z, length_r), F32),
            pltpu.VMEM((2, 4, length_z, length_r), F32),
            pltpu.VMEM((2, 4, length_a, length_r), F32),
            pltpu.VMEM((2, 4, length_a, length_r), F32),
            dma((2,)),
            dma,
            dma((n_xs // GROUP,)),
            dma((2,)),
            dma((2,)),
            dma((4,)),
            dma((4,)),
        ],
        compiler_params=pltpu.CompilerParams(
            collective_id=0, has_side_effects=True, vmem_limit_bytes=40 * 1024 * 1024
        ),
    )(
        bubble_part.reshape(1, held),
        bubble_elem.reshape(1, held),
        bubble_ref,
        bubble_vel,
        inv_tau.reshape(1, held),
        basset_coef.reshape(1, held),
        scale,
        const,
        quad,
        velocity,
        history.transpose(1, 0, 2).reshape(3 * steps, held),
    )


def solution(mesh):
    return jax.shard_map(
        shards,
        mesh=mesh,
        in_specs=(
            P(None, "ax", "xs", None),
            P(None, "ax", "xs", None),
            P(("ax", "xs")),
            P(("ax", "xs")),
            P(None, ("ax", "xs")),
            P(None, ("ax", "xs")),
            P(("ax", "xs")),
            P(("ax", "xs")),
            P(None, None, ("ax", "xs")),
        ),
        out_specs=(P(None, "ax", "xs", None), P(None, ("ax", "xs"))),
        check_vma=False,
    )
```

time: 35.4 us -> 31.2 us (0.88)
  Pallas kernels: 29.6 us -> 26 us
  local copies, waits for them, and re-layouts: 4.86 us -> 4.15 us
    pallas_call x1, Pallas kernels: 29.6 us -> 26 us  [shards(): pl.pallas_call(functools.partial(kernel, n_ax, n_xs), out_shape=(jax.Shap...]
    reshape x1 -> x0, local copies, waits for them, and re-layouts: 0.69 us -> none  [shards(): history.reshape(3 * steps, held)]
    unnamed x23 -> x24, local copies, waits for them, and re-layouts: 3.97 us -> 3.96 us
where the time goes in v2:
time: 31.2 us; the launch traced here: 31 us
  Pallas kernels  26 us (83%)
  local copies, waits for them, and re-layouts  4.15 us (13%)
  between operations  0.76 us (2%)
    pallas_call x1, Pallas kernels, shards(): pl.pallas_call(functools.partial(kernel, n_ax, n_xs), out_shape=(jax.Shap...  26 us
    unnamed x24, local copies, waits for them, and re-layouts  3.96 us

profile of v2, /device:TPU:1, one launch (start us, length us, event | category | flops | bytes accessed | tf_op | source)
XLA Modules:
  0.0 31.0 jit_solution(5367336069215703985)
XLA Ops:
  0.6 0.0 copy-start
  0.6 0.0 copy-start.2
  0.7 0.7 %copy-done = f32[3,1,4,16]{3,2,1,0:T(4,128)S(1)} copy-done((f32[3,1,4,16]{3,2,1,0:T(4,128)S(1)}, f32[3,1,4,16]{3,2,1,0:T(4,128)}, u32[]{:S(2)}) %copy-start) | copy-done | bytes 792
  1.3 0.1 copy.15
  1.4 0.0 copy-start.3
  1.4 0.0 copy-start.4
  1.5 0.0 copy-start.5
  1.5 0.0 copy-start.6
  1.5 0.0 copy-start.7
  1.5 0.0 copy-start.8
  1.5 0.0 copy-start.9
  1.5 0.0 copy-start.10
  1.5 0.1 copy.16.scale_ref
  1.6 0.0 copy-done.2
  1.6 0.7 %copy-done.3 = f32[240,128]{1,0:T(8,128)S(1)} copy-done((f32[240,128]{1,0:T(8,128)S(1)}, f32[240,128]{1,0:T(8,128)}, u32[]{:S(2)}) %copy-start.3) | copy-done | bytes 122904
  2.4 0.0 copy-done.4
  2.4 0.0 copy-done.5
  2.4 0.0 copy-done.6
  2.4 0.0 copy-done.7
  2.4 0.0 copy-done.8
  2.4 0.0 copy-done.9
  2.4 0.0 copy-done.10
  2.4 0.0 copy-start.1
  2.4 1.1 %copy-done.1 = bf16[128,3,1024]{2,0,1:T(8,128)(2,1)S(1)} copy-done((bf16[128,3,1024]{2,0,1:T(8,128)(2,1)S(1)}, bf16[128,3,1024]{2,0,1:T(8,128)(2,1)}, u32[]{:S(2)}) %copy-start.1) | copy-done | bytes 786456
  3.5 26.0 %shard_map.122 = (f32[3,8,32,128]{3,2,1,0:T(8,128)S(1)}, f32[3,1024]{1,0:T(4,128)S(1)}) custom-call(s32[1,1024]{1,0:T(1,128)S(1)} %bitcast.14, s32[1,1024]{1,0:T(1,128)S(1)} %bitcast.15, f32[3,1024]{1,0:T(4,128)S(1)} %copy-done.4, f32[3,1024]{1,0:T(4,128)S(1)} %copy-done.5, f32[1,1024]{1,0:T(1,128)S(1)} %bitcast.16, f32[1,1024]{1,0:T(1,128)S(1)} %bitcast.17, ...), custom_call_target="tpu_custom_call" | custom-call | tf_op jit(solution)/shard_map/pallas_call | solution.py:421
  29.6 0.7 %copy.19 = f32[3,8,32,128]{3,2,1,0:T(8,128)} copy(f32[3,8,32,128]{3,2,1,0:T(8,128)S(1)} %get-tuple-element.4) | data formatting | bytes 786432
  30.4 0.6 %copy.20 = f32[3,1024]{1,0:T(4,128)} copy(f32[3,1024]{1,0:T(4,128)S(1)} %get-tuple-element.5) | data formatting | bytes 24576
  (2 shorter events, 0.0 us)
Async XLA Ops:
  0.6 0.7 %copy-start = (f32[3,1,4,16]{3,2,1,0:T(4,128)S(1)}, f32[3,1,4,16]{3,2,1,0:T(4,128)}, u32[]{:S(2)}) copy-start(f32[3,1,4,16]{3,2,1,0:T(4,128)} %param.12) | copy-start | bytes 2308
  0.6 1.0 %copy-start.2 = (f32[3,8,32,128]{3,2,1,0:T(8,128)S(1)}, f32[3,8,32,128]{3,2,1,0:T(8,128)}, u32[]{:S(2)}) copy-start(f32[3,8,32,128]{3,2,1,0:T(8,128)} %vel_hbm.1) | copy-start | bytes 1179652
  1.4 0.9 %copy-start.3 = (f32[240,128]{1,0:T(8,128)S(1)}, f32[240,128]{1,0:T(8,128)}, u32[]{:S(2)}) copy-start(f32[240,128]{1,0:T(8,128)} %constant.4.clone.const_ref) | copy-start | bytes 368644
  1.4 0.9 %copy-start.4 = (f32[3,1024]{1,0:T(4,128)S(1)}, f32[3,1024]{1,0:T(4,128)}, u32[]{:S(2)}) copy-start(f32[3,1024]{1,0:T(4,128)} %ref_ref.1) | copy-start | bytes 36868
  1.5 0.9 %copy-start.5 = (f32[3,1024]{1,0:T(4,128)S(1)}, f32[3,1024]{1,0:T(4,128)}, u32[]{:S(2)}) copy-start(f32[3,1024]{1,0:T(4,128)} %bvel_ref.1) | copy-start | bytes 36868
  1.5 0.9 %copy-start.6 = (bf16[16,384]{1,0:T(8,128)(2,1)S(1)}, bf16[16,384]{1,0:T(8,128)(2,1)}, u32[]{:S(2)}) copy-start(bf16[16,384]{1,0:T(8,128)(2,1)} %constant.5.clone.quad_ref) | copy-start | bytes 36868
  1.5 0.9 %copy-start.7 = (s32[1024]{0:T(1024)S(1)}, s32[1024]{0:T(1024)}, u32[]{:S(2)}) copy-start(s32[1024]{0:T(1024)} %param.13) | copy-start | bytes 12292
  1.5 0.9 %copy-start.8 = (s32[1024]{0:T(1024)S(1)}, s32[1024]{0:T(1024)}, u32[]{:S(2)}) copy-start(s32[1024]{0:T(1024)} %param.14) | copy-start | bytes 12292
  1.5 0.9 %copy-start.9 = (f32[1024]{0:T(1024)S(1)}, f32[1024]{0:T(1024)}, u32[]{:S(2)}) copy-start(f32[1024]{0:T(1024)} %param.17) | copy-start | bytes 12292
  1.5 0.9 %copy-start.10 = (f32[1024]{0:T(1024)S(1)}, f32[1024]{0:T(1024)}, u32[]{:S(2)}) copy-start(f32[1024]{0:T(1024)} %param.18) | copy-start | bytes 12292
  2.4 1.1 %copy-start.1 = (bf16[128,3,1024]{2,0,1:T(8,128)(2,1)S(1)}, bf16[128,3,1024]{2,0,1:T(8,128)(2,1)}, u32[]{:S(2)}) copy-start(bf16[128,3,1024]{2,0,1:T(8,128)(2,1)} %param.19) | copy-start | bytes 2359300

commit v3 on v2

--- a/solution.py
+++ b/solution.py
@@ -52,9 +52,10 @@
 ROW_ROLL = 16
 ROW_WEIGHT = 80
 ROW_RADIAL = 112
-
-
-def constant_table():
+ROW_QUAD = 240
+
+
+def constant_table(steps):
     points = np.array(GLL_POINTS)
     weights = np.array(GLL_WEIGHTS)
     rows = [np.repeat(points[:, None], 128, axis=1)]
@@ -65,16 +66,32 @@
         rows.append(np.repeat(coef[:, None], 128, axis=1))
     rows.append(np.tile(weights, 4)[:, None] * np.tile(weights, 16)[None, :])
     rows.append(np.kron(np.eye(16), DMAT.T))
+    rows += quadrature_rows(steps)
     return np.concatenate(rows, axis=0).astype(np.float32)
 
 
 def quadrature_rows(length):
     steps = np.arange(length, dtype=np.float32)
     quad = np.sqrt(steps + np.float32(1.0)) - np.sqrt(steps)
-    rows = np.zeros((16, 3, length), np.float32)
+    rows = np.zeros((3, 8, length), np.float32)
     for comp in range(3):
         rows[comp, comp] = quad
-    return rows.reshape(16, 3 * length)
+    return list(rows)
+
+
+def peers_by_distance(n_xs):
+    length_x, length_y, cores = {32: (4, 4, 2), 4: (2, 1, 2)}[n_xs]
+    offsets = [
+        (dx, dy, core)
+        for dx in range(length_x)
+        for dy in range(length_y)
+        for core in range(cores)
+    ]
+
+    def distance(offset):
+        return min(offset[0], length_x - offset[0]) + min(offset[1], length_y - offset[1])
+
+    return (length_x, length_y, cores), sorted(offsets, key=distance)
 
 
 def split3(values):
@@ -112,7 +129,7 @@
     ).astype(F32).astype(BF16)
 
 
-def dispatch(rel, n_xs, coords, elem, lhs, onehot, sendq, recvq):
+def dispatch(rel, codes, coords, elem, lhs, onehot, sendq, recvq):
     held = rel.shape[1]
     high, mid, low = split3(coords)
     packed = jnp.concatenate(
@@ -120,8 +137,9 @@
     ).astype(BF16)
     rel16 = jnp.broadcast_to(rel, (16, held))
     zero = jnp.zeros((16, held), BF16)
-    for step in range(n_xs):
-        lhs[16 * step : 16 * step + 16, :] = jnp.where(rel16 == step, packed, zero)
+    n_xs = len(codes)
+    for place, code in enumerate(codes):
+        lhs[16 * place : 16 * place + 16, :] = jnp.where(rel16 == code, packed, zero)
     slots = lax.dot_general(
         lhs[...], onehot[...], (((1,), (1,)), ((), ())), preferred_element_type=F32
     ).reshape(n_xs, 2, 8, SLOTS)
@@ -133,7 +151,7 @@
     recvq[0] = slots[0]
 
 
-def advection(vel_ref, scale_ref, const_ref, table, wsum):
+def advection(vel_ref, metric_ref, const_ref, table, wsum):
     vel = vel_ref[...]
     length_a, length_r = vel.shape[2], vel.shape[3]
     nodes = 8 * length_a
@@ -143,7 +161,24 @@
         preferred_element_type=F32,
         precision=lax.Precision.HIGHEST,
     ).reshape(vel.shape)
-    scale = scale_ref[...]
+    spread = (
+        lax.broadcasted_iota(jnp.int32, (length_r // 8, length_r), 1) // 8
+        == lax.broadcasted_iota(jnp.int32, (length_r // 8, length_r), 0)
+    ).astype(F32)
+    scale = []
+    for factor in range(3):
+        rows = jnp.dot(
+            metric_ref[factor], spread, preferred_element_type=F32, precision=lax.Precision.HIGHEST
+        )
+        scale.append(
+            jnp.concatenate(
+                [
+                    jnp.broadcast_to(rows[e : e + 1], (8, length_r))
+                    for e in range(length_a // 8)
+                ],
+                axis=0,
+            )
+        )
     inverse = const_ref[ROW_WEIGHT : ROW_WEIGHT + 32, :] / (scale[0] * scale[1] * scale[2])
     lane = lax.broadcasted_iota(jnp.int32, (4, length_a, length_r), 2)
     upper = (lane % 8 == 7) & (lane < length_r - 1)
@@ -252,8 +287,10 @@
     ]
 
 
-def gather(rel8, n_xs, recvr, onehot):
-    held = rel8.shape[1]
+def gather(rel, codes, recvr, onehot):
+    held = rel.shape[1]
+    n_xs = len(codes)
+    rel8 = jnp.broadcast_to(rel, (8, held))
     answers = recvr[...].reshape(4 * n_xs, SLOTS)
     spread = jnp.dot(
         jnp.concatenate([p.astype(BF16) for p in split3(answers)], axis=0),
@@ -261,42 +298,74 @@
         preferred_element_type=F32,
     )
     span = 4 * n_xs
-    half = lax.broadcasted_iota(jnp.int32, (8, held), 0) // 4
+    half = lax.broadcasted_iota(jnp.int32, (8, held), 0) < 4
     total = jnp.zeros((8, held), F32)
     for pair in range(n_xs // 2):
         rows = [spread[w * span + 8 * pair : w * span + 8 * pair + 8] for w in range(3)]
-        total = total + jnp.where(rel8 - half == 2 * pair, rows[0] + rows[1] + rows[2], 0.0)
+        code = jnp.where(half, codes[2 * pair], codes[2 * pair + 1])
+        total = total + jnp.where(rel8 == code, rows[0] + rows[1] + rows[2], 0.0)
     total = total + pltpu.roll(total, 4, 0)
     return total[0:3]
 
 
 def kernel(
     n_ax, n_xs,
-    part_ref, elem_ref, ref_ref, bvel_ref, tau_ref, coef_ref, scale_ref, const_ref, quad_ref,
-    vel_hbm, hist_hbm,
-    fluid_ref, bubble_ref,
-    vel_ref, hist_ref, lhs, onehot, sendq, recvq, sendr, recvr, table, wsum,
-    face_out, face_in, plane_out, plane_in,
+    part_hbm, elem_hbm, ref_hbm, tau_hbm, vel_hbm, metric_hbm, const_hbm, bvel_hbm, coef_hbm,
+    hist_hbm,
+    fluid_hbm, bubble_ref,
+    part_ref, elem_ref, ref_ref, tau_ref, vel_ref, metric_ref, const_ref, bvel_ref, coef_ref,
+    hist_ref,
+    fluid_ref, lhs, onehot, sendq, recvq, sendr, recvr, table, wsum, face_out, face_in, plane_out, plane_in,
     local_sem, q_send, q_recv, r_send, r_recv, h_send, h_recv,
 ):
     ax = lax.axis_index("ax")
     me = lax.axis_index("xs")
     held = part_ref.shape[1]
-    up, down = lax.rem(ax + 1, n_ax), lax.rem(ax + n_ax - 1, n_ax)
-
-    load_vel = pltpu.make_async_copy(vel_hbm, vel_ref, local_sem.at[0])
-    load_vel.start()
-    load_hist = pltpu.make_async_copy(hist_hbm, hist_ref, local_sem.at[1])
-    load_hist.start()
-
-    def wrap(place):
-        return jnp.where(place >= n_xs, place - n_xs, place)
+    (length_x, length_y, cores), offsets = peers_by_distance(n_xs)
+    codes = [(dx * length_y + dy) * cores + core for dx, dy, core in offsets]
+
+    loads = [
+        pltpu.make_async_copy(source, target, local_sem.at[i])
+        for i, (source, target) in enumerate(
+            [
+                (part_hbm, part_ref), (elem_hbm, elem_ref), (ref_hbm, ref_ref),
+                (tau_hbm, tau_ref), (vel_hbm, vel_ref), (metric_hbm, metric_ref),
+                (const_hbm, const_ref), (bvel_hbm, bvel_ref), (coef_hbm, coef_ref),
+                (hist_hbm, hist_ref),
+            ]
+        )
+    ]
+    for load in loads:
+        load.start()
+
+    def wrap(place, length):
+        return jnp.where(place >= length, place - length, place)
+
+    here_x = lax.div(me, length_y * cores)
+    here_y = lax.rem(lax.div(me, cores), length_y)
+    here_core = lax.rem(me, cores)
+    places_x = [wrap(here_x + d, length_x) * (length_y * cores) for d in range(length_x)]
+    places_y = [wrap(here_y + d, length_y) * cores for d in range(length_y)]
+    places_core = [wrap(here_core + d, cores) for d in range(cores)]
+
+    def ahead(place):
+        dx, dy, core = offsets[place]
+        return places_x[dx] + places_y[dy] + places_core[core]
+
+    def behind(place):
+        dx, dy, core = offsets[place]
+        return (
+            places_x[(length_x - dx) % length_x]
+            + places_y[(length_y - dy) % length_y]
+            + places_core[(cores - core) % cores]
+        )
+
+    up, down = wrap(ax + 1, n_ax), wrap(ax + n_ax - 1, n_ax)
+    left, right = wrap(me + n_xs - 1, n_xs), wrap(me + 1, n_xs)
 
     barrier = pltpu.get_barrier_semaphore()
-    for step in range(1, n_xs):
-        pl.semaphore_signal(
-            barrier, inc=1, device_id=(ax, wrap(me + step)), device_id_type=MESH
-        )
+    for place in range(n_xs - 1, 0, -1):
+        pl.semaphore_signal(barrier, inc=1, device_id=(ax, behind(place)), device_id_type=MESH)
     for other in (up, down):
         pl.semaphore_signal(barrier, inc=1, device_id=(other, me), device_id_type=MESH)
 
@@ -310,13 +379,13 @@
             device_id_type=MESH,
         )
 
-    def answer_copy(tile, count, odd, step):
+    def answer_copy(tile, count, odd, target):
         return pltpu.make_async_remote_copy(
             src_ref=sendr.at[pl.ds(tile, count), pl.ds(4 * odd, 3)],
             dst_ref=recvr.at[pl.ds(tile, count), pl.ds(4 * odd, 3)],
             send_sem=r_send.at[odd],
             recv_sem=r_recv.at[odd],
-            device_id=(ax, wrap(me + n_xs - step)),
+            device_id=(ax, target),
             device_id_type=MESH,
         )
 
@@ -326,7 +395,7 @@
             dst_ref=face_in.at[side],
             send_sem=h_send.at[side],
             recv_sem=h_recv.at[side],
-            device_id=(ax, wrap(me + (1 if side == 0 else n_xs - 1))),
+            device_id=(ax, right if side == 0 else left),
             device_id_type=MESH,
         )
 
@@ -340,68 +409,87 @@
             device_id_type=MESH,
         )
 
-    rel = part_ref[...] - me
-    rel = jnp.where(rel < 0, rel + n_xs, rel)
+    for load in loads[0:4]:
+        load.wait()
+    part = part_ref[...]
+    far_x = part // (length_y * cores) - here_x
+    far_y = (part // cores) % length_y - here_y
+    far_core = part % cores - here_core
+    rel = (
+        jnp.where(far_x < 0, far_x + length_x, far_x) * (length_y * cores)
+        + jnp.where(far_y < 0, far_y + length_y, far_y) * cores
+        + jnp.where(far_core < 0, far_core + cores, far_core)
+    )
     ranked(rel, n_xs, onehot)
     coords = jnp.concatenate([ref_ref[...], tau_ref[...]], axis=0)
-    dispatch(rel, n_xs, coords, elem_ref[...].astype(F32), lhs, onehot, sendq, recvq)
+    dispatch(rel, codes, coords, elem_ref[...].astype(F32), lhs, onehot, sendq, recvq)
+    for load in loads[4:7]:
+        load.wait()
+    advection(vel_ref, metric_ref, const_ref, table, wsum)
+    azimuth_pairs(wsum, face_out)
     pl.semaphore_wait(barrier, n_xs + 1)
-    for step in range(1, n_xs):
-        query_copy(step, 1, (step - 1) // GROUP, wrap(me + step)).start()
-
-    load_vel.wait()
-    advection(vel_ref, scale_ref, const_ref, table, wsum)
-    azimuth_pairs(wsum, face_out)
     for side in range(2):
         face_copy(side).start()
-
-    def serve(group, count):
-        first = GROUP * group + 1
-        query_copy(first, count, group, me).wait_recv()
-        sources = [recvq[first + i] for i in range(count)]
-        if count < GROUP:
-            sources.append(recvq[0])
+    for place in range(n_xs - 1, 0, -1):
+        query_copy(place, 1, place // GROUP, ahead(place)).start()
+
+    groups = n_xs // GROUP
+    for group in range(groups):
+        if group == min(3, groups - 1):
+            for side in range(2):
+                face_copy(side).wait()
+            add_faces(wsum, face_in, plane_out)
+            for side in range(2):
+                plane_copy(side).start()
+        first = GROUP * group
+        skip = 1 if group == 0 else 0
+        query_copy(first + skip, GROUP - skip, group, me).wait_recv()
+        sources = [recvq[first + i] for i in range(GROUP)]
         values = interpolate(jnp.concatenate(sources, axis=1), const_ref, table)
         for i in range(GROUP):
+            place = first + i
             lanes = slice(SLOTS * i, SLOTS * (i + 1))
-            if i == count:
-                for comp in range(3):
-                    recvr[0, comp : comp + 1, :] = values[comp][:, lanes]
-            else:
-                tile, odd = (GROUP // 2) * group + (1 + i) // 2, (1 + i) % 2
-                for comp in range(3):
-                    row = 4 * odd + comp
-                    sendr[tile, row : row + 1, :] = values[comp][:, lanes]
-                answer_copy(tile, 1, odd, first + i).start()
-
-    groups = n_xs // GROUP
-
-    def serve_step(group, carry):
-        serve(group, GROUP)
-        return carry
-
-    lax.fori_loop(0, groups - 1, serve_step, 0)
-    serve(groups - 1, GROUP - 1)
-
-    for side in range(2):
-        face_copy(side).wait()
-    add_faces(wsum, face_in, plane_out)
-    for side in range(2):
-        plane_copy(side).start()
-
-    load_hist.wait()
-    basset = jnp.dot(quad_ref[...], hist_ref[...], preferred_element_type=F32)[0:3]
+            target = sendr if place > 0 else recvr
+            for comp in range(3):
+                row = 4 * (place % 2) + comp
+                target[place // 2, row : row + 1, :] = values[comp][:, lanes]
+            if place > 0:
+                answer_copy(place // 2, 1, place % 2, behind(place)).start()
+
+    for load in loads[7:]:
+        load.wait()
+    quad = jnp.concatenate(
+        [const_ref[ROW_QUAD + 8 * comp : ROW_QUAD + 8 * comp + 8, :] for comp in range(3)], axis=1
+    )
+    quad = jnp.concatenate([quad, jnp.zeros_like(quad)], axis=0).astype(BF16)
+    basset = jnp.dot(quad, hist_ref[...], preferred_element_type=F32)[0:3]
     local = coef_ref[...] * basset - tau_ref[...] * bvel_ref[...]
 
     for side in range(2):
         plane_copy(side).wait()
     fluid_finish(wsum, plane_in, fluid_ref)
+    store_fluid = pltpu.make_async_copy(fluid_ref, fluid_hbm, local_sem.at[len(loads)])
+    store_fluid.start()
 
     query_copy(1, n_xs - 1, 0, me).wait_send()
-    answer_copy(1, n_xs // 2 - 1, 0, 0).wait()
-    answer_copy(0, n_xs // 2, 1, 0).wait()
-    rel8 = jnp.broadcast_to(rel, (8, held))
-    bubble_ref[...] = gather(rel8, n_xs, recvr, onehot) + local
+    answer_copy(1, n_xs // 2 - 1, 0, me).wait()
+    answer_copy(0, n_xs // 2, 1, me).wait()
+    bubble_ref[...] = gather(rel, codes, recvr, onehot) + local
+    store_fluid.wait()
+
+
+def store(fluid_in, bubble_in, fluid_out, bubble_out, fluid_ref, bubble_ref, in_sems, out_sems):
+    pieces = [(fluid_in.at[c], fluid_ref.at[c], fluid_out.at[c]) for c in range(3)]
+    pieces.append((bubble_in, bubble_ref, bubble_out))
+    reads = [pltpu.make_async_copy(p[0], p[1], in_sems.at[i]) for i, p in enumerate(pieces)]
+    writes = [pltpu.make_async_copy(p[1], p[2], out_sems.at[i]) for i, p in enumerate(pieces)]
+    for read in reads:
+        read.start()
+    for read, write in zip(reads, writes):
+        read.wait()
+        write.start()
+    for write in writes:
+        write.wait()
 
 
 def shards(
@@ -412,23 +500,33 @@
     held = bubble_part.shape[0]
     steps = history.shape[0]
     _, length_z, length_a, length_r = velocity.shape
-    scale = jnp.repeat(jnp.repeat(metric[:, 0], 8, axis=1), 8, axis=2)
-    const = jnp.asarray(constant_table())
-    quad = jnp.asarray(quadrature_rows(steps), BF16)
     vmem = pl.BlockSpec(memory_space=pltpu.VMEM)
     anywhere = pl.BlockSpec(memory_space=pl.ANY)
     dma = pltpu.SemaphoreType.DMA
-    return pl.pallas_call(
+    outputs = (
+        jax.ShapeDtypeStruct(velocity.shape, F32),
+        jax.ShapeDtypeStruct((3, held), F32),
+    )
+    operands = [
+        bubble_part.reshape(1, held),
+        bubble_elem.reshape(1, held),
+        bubble_ref,
+        inv_tau.reshape(1, held),
+        velocity,
+        metric.reshape(3, length_a // 8, length_r // 8),
+        jnp.asarray(constant_table(steps)),
+        bubble_vel,
+        basset_coef.reshape(1, held),
+        history.transpose(1, 0, 2).reshape(3 * steps, held),
+    ]
+    results = pl.pallas_call(
         functools.partial(kernel, n_ax, n_xs),
-        out_shape=(
-            jax.ShapeDtypeStruct(velocity.shape, F32),
-            jax.ShapeDtypeStruct((3, held), F32),
-        ),
-        in_specs=[vmem] * 9 + [anywhere] * 2,
-        out_specs=(vmem, vmem),
-        scratch_shapes=[
+        out_shape=outputs,
+        in_specs=[anywhere] * len(operands),
+        out_specs=(anywhere, vmem),
+        scratch_shapes=[pltpu.VMEM(o.shape, o.dtype) for o in operands]
+        + [
             pltpu.VMEM(velocity.shape, F32),
-            pltpu.VMEM((3 * steps, held), BF16),
             pltpu.VMEM((16 * n_xs, held), BF16),
             pltpu.VMEM((SLOTS, held), BF16),
             pltpu.VMEM((n_xs, 8, SLOTS), F32),
@@ -441,7 +539,7 @@
             pltpu.VMEM((2, 4, length_z, length_r), F32),
             pltpu.VMEM((2, 4, length_a, length_r), F32),
             pltpu.VMEM((2, 4, length_a, length_r), F32),
-            dma((2,)),
+            dma((len(operands) + 1,)),
             dma,
             dma((n_xs // GROUP,)),
             dma((2,)),
@@ -450,21 +548,17 @@
             dma((4,)),
         ],
         compiler_params=pltpu.CompilerParams(
-            collective_id=0, has_side_effects=True, vmem_limit_bytes=40 * 1024 * 1024
+            collective_id=0, has_side_effects=True, vmem_limit_bytes=56 * 1024 * 1024
         ),
-    )(
-        bubble_part.reshape(1, held),
-        bubble_elem.reshape(1, held),
-        bubble_ref,
-        bubble_vel,
-        inv_tau.reshape(1, held),
-        basset_coef.reshape(1, held),
-        scale,
-        const,
-        quad,
-        velocity,
-        history.transpose(1, 0, 2).reshape(3 * steps, held),
-    )
+    )(*operands)
+    return pl.pallas_call(
+        store,
+        out_shape=outputs,
+        in_specs=[anywhere, anywhere],
+        out_specs=(anywhere, anywhere),
+        scratch_shapes=[pltpu.VMEM(o.shape, o.dtype) for o in outputs] + [dma((4,)), dma((4,))],
+        compiler_params=pltpu.CompilerParams(vmem_limit_bytes=56 * 1024 * 1024),
+    )(*results)
 
 
 def solution(mesh):

time: 31.2 us -> 28.9 us (0.926)
  local copies, waits for them, and re-layouts: 4.15 us -> 0 us
  Pallas kernels: 26 us -> 28.1 us
    unnamed x24 -> x0, local copies, waits for them, and re-layouts: 3.96 us -> none
    pallas_call x1 -> x2, Pallas kernels: 26 us -> 28.1 us  [the longest x1 26.3 us: shards(): pl.pallas_call(functools.partial(kernel, n_ax, n_xs), out_shape=outputs,...]
where the time goes in v3:
time: 28.9 us; the launch traced here: 28.7 us
  Pallas kernels  28.1 us (97%)
  between operations  0.64 us (2%)
    pallas_call x1, Pallas kernels, shards(): pl.pallas_call(functools.partial(kernel, n_ax, n_xs), out_shape=outputs,...  26.3 us
    pallas_call x1, Pallas kernels, shards(): pl.pallas_call(store, out_shape=outputs, in_specs=[anywhere, anywhere], o...  1.76 us

profile of v3, /device:TPU:1, one launch (start us, length us, event | category | flops | bytes accessed | tf_op | source)
XLA Modules:
  0.0 28.7 jit_solution(17422848339012204920)
XLA Ops:
  0.6 26.3 %shard_map.113 = (f32[3,8,32,128]{3,2,1,0:T(8,128)}, f32[3,1024]{1,0:T(4,128)}) custom-call(s32[1,1024]{1,0:T(1,128)} %bitcast.10, s32[1,1024]{1,0:T(1,128)} %bitcast.11, f32[3,1024]{1,0:T(4,128)} %ref_hbm.1, f32[1,1024]{1,0:T(1,128)} %bitcast.12, f32[3,8,32,128]{3,2,1,0:T(8,128)} %vel_hbm.1, f32[3,4,16]{2,1,0:T(4,128)} %bitcast.9, ...), custom_call_target="tpu_custom_call" | custom-call | tf_op jit(solution)/shard_map/pallas_call | solution.py:522
  27.0 1.8 %shard_map.114 = (f32[3,8,32,128]{3,2,1,0:T(8,128)}, f32[3,1024]{1,0:T(4,128)}) custom-call(f32[3,8,32,128]{3,2,1,0:T(8,128)} %get-tuple-element.4.fluid_in, f32[3,1024]{1,0:T(4,128)} %get-tuple-element.5.bubble_in), custom_call_target="tpu_custom_call" | custom-call | tf_op jit(solution)/shard_map/pallas_call | solution.py:554

commit v4 on v3

--- a/solution.py
+++ b/solution.py
@@ -335,7 +335,7 @@
             ]
         )
     ]
-    for load in loads:
+    for load in loads[0:4]:
         load.start()
 
     def wrap(place, length):
@@ -408,6 +408,9 @@
             device_id=(up if side == 0 else down, me),
             device_id_type=MESH,
         )
+
+    for load in loads[4:]:
+        load.start()
 
     for load in loads[0:4]:
         load.wait()
@@ -423,19 +426,22 @@
     ranked(rel, n_xs, onehot)
     coords = jnp.concatenate([ref_ref[...], tau_ref[...]], axis=0)
     dispatch(rel, codes, coords, elem_ref[...].astype(F32), lhs, onehot, sendq, recvq)
+    pl.semaphore_wait(barrier, n_xs + 1)
+    for place in range(n_xs - 1, 0, -1):
+        query_copy(place, 1, place // GROUP, ahead(place)).start()
     for load in loads[4:7]:
         load.wait()
     advection(vel_ref, metric_ref, const_ref, table, wsum)
     azimuth_pairs(wsum, face_out)
-    pl.semaphore_wait(barrier, n_xs + 1)
     for side in range(2):
         face_copy(side).start()
-    for place in range(n_xs - 1, 0, -1):
-        query_copy(place, 1, place // GROUP, ahead(place)).start()
 
     groups = n_xs // GROUP
-    for group in range(groups):
-        if group == min(3, groups - 1):
+    middle = groups // 4
+    order = list(range(middle, groups - 3))
+    order += [g for g in range(groups - 1, -1, -1) if g not in order]
+    for turn, group in enumerate(order):
+        if turn == min(3, groups - 1):
             for side in range(2):
                 face_copy(side).wait()
             add_faces(wsum, face_in, plane_out)

time: 28.9 us -> 27.9 us (0.965)
  Pallas kernels: 28.1 us -> 27.1 us
    pallas_call x1, Pallas kernels: 26.3 us -> 25.4 us  [shards(): pl.pallas_call(functools.partial(kernel, n_ax, n_xs), out_shape=outputs,...]
where the time goes in v4:
time: 27.9 us; the launch traced here: 27.8 us
  Pallas kernels  27.1 us (97%)
  between operations  0.64 us (2%)
    pallas_call x1, Pallas kernels, shards(): pl.pallas_call(functools.partial(kernel, n_ax, n_xs), out_shape=outputs,...  25.4 us
    pallas_call x1, Pallas kernels, shards(): pl.pallas_call(store, out_shape=outputs, in_specs=[anywhere, anywhere], o...  1.76 us

profile of v4, /device:TPU:1, one launch (start us, length us, event | category | flops | bytes accessed | tf_op | source)
XLA Modules:
  0.0 27.8 jit_solution(8353260411591969768)
XLA Ops:
  0.6 25.4 %shard_map.113 = (f32[3,8,32,128]{3,2,1,0:T(8,128)}, f32[3,1024]{1,0:T(4,128)}) custom-call(s32[1,1024]{1,0:T(1,128)} %bitcast.10, s32[1,1024]{1,0:T(1,128)} %bitcast.11, f32[3,1024]{1,0:T(4,128)} %ref_hbm.1, f32[1,1024]{1,0:T(1,128)} %bitcast.12, f32[3,8,32,128]{3,2,1,0:T(8,128)} %vel_hbm.1, f32[3,4,16]{2,1,0:T(4,128)} %bitcast.9, ...), custom_call_target="tpu_custom_call" | custom-call | tf_op jit(solution)/shard_map/pallas_call | solution.py:528
  26.0 1.8 %shard_map.114 = (f32[3,8,32,128]{3,2,1,0:T(8,128)}, f32[3,1024]{1,0:T(4,128)}) custom-call(f32[3,8,32,128]{3,2,1,0:T(8,128)} %get-tuple-element.4.fluid_in, f32[3,1024]{1,0:T(4,128)} %get-tuple-element.5.bubble_in), custom_call_target="tpu_custom_call" | custom-call | tf_op jit(solution)/shard_map/pallas_call | solution.py:560

commit v5 on v4

--- a/solution.py
+++ b/solution.py
@@ -335,9 +335,6 @@
             ]
         )
     ]
-    for load in loads[0:4]:
-        load.start()
-
     def wrap(place, length):
         return jnp.where(place >= length, place - length, place)
 
@@ -364,10 +361,10 @@
     left, right = wrap(me + n_xs - 1, n_xs), wrap(me + 1, n_xs)
 
     barrier = pltpu.get_barrier_semaphore()
+    for other in (up, down):
+        pl.semaphore_signal(barrier, inc=1, device_id=(other, me), device_id_type=MESH)
     for place in range(n_xs - 1, 0, -1):
         pl.semaphore_signal(barrier, inc=1, device_id=(ax, behind(place)), device_id_type=MESH)
-    for other in (up, down):
-        pl.semaphore_signal(barrier, inc=1, device_id=(other, me), device_id_type=MESH)
 
     def query_copy(first, count, group, target):
         return pltpu.make_async_remote_copy(
@@ -409,7 +406,7 @@
             device_id_type=MESH,
         )
 
-    for load in loads[4:]:
+    for load in loads:
         load.start()
 
     for load in loads[0:4]:

time: 27.9 us -> 27.7 us (level)
  no operation moved by 1% of the time
where the time goes in v5:
time: 27.7 us; the launch traced here: 27.5 us
  Pallas kernels  26.9 us (97%)
  between operations  0.64 us (2%)
    pallas_call x1, Pallas kernels, shards(): pl.pallas_call(functools.partial(kernel, n_ax, n_xs), out_shape=outputs,...  25.1 us
    pallas_call x1, Pallas kernels, shards(): pl.pallas_call(store, out_shape=outputs, in_specs=[anywhere, anywhere], o...  1.76 us

profile of v5, /device:TPU:1, one launch (start us, length us, event | category | flops | bytes accessed | tf_op | source)
XLA Modules:
  0.0 27.5 jit_solution(13372043716900490259)
XLA Ops:
  0.6 25.1 %shard_map.113 = (f32[3,8,32,128]{3,2,1,0:T(8,128)}, f32[3,1024]{1,0:T(4,128)}) custom-call(s32[1,1024]{1,0:T(1,128)} %bitcast.10, s32[1,1024]{1,0:T(1,128)} %bitcast.11, f32[3,1024]{1,0:T(4,128)} %ref_hbm.1, f32[1,1024]{1,0:T(1,128)} %bitcast.12, f32[3,8,32,128]{3,2,1,0:T(8,128)} %vel_hbm.1, f32[3,4,16]{2,1,0:T(4,128)} %bitcast.9, ...), custom_call_target="tpu_custom_call" | custom-call | tf_op jit(solution)/shard_map/pallas_call | solution.py:525
  25.8 1.8 %shard_map.114 = (f32[3,8,32,128]{3,2,1,0:T(8,128)}, f32[3,1024]{1,0:T(4,128)}) custom-call(f32[3,8,32,128]{3,2,1,0:T(8,128)} %get-tuple-element.4.fluid_in, f32[3,1024]{1,0:T(4,128)} %get-tuple-element.5.bubble_in), custom_call_target="tpu_custom_call" | custom-call | tf_op jit(solution)/shard_map/pallas_call | solution.py:557

commit v6 on v5

--- a/solution.py
+++ b/solution.py
@@ -423,13 +423,13 @@
     ranked(rel, n_xs, onehot)
     coords = jnp.concatenate([ref_ref[...], tau_ref[...]], axis=0)
     dispatch(rel, codes, coords, elem_ref[...].astype(F32), lhs, onehot, sendq, recvq)
-    pl.semaphore_wait(barrier, n_xs + 1)
-    for place in range(n_xs - 1, 0, -1):
-        query_copy(place, 1, place // GROUP, ahead(place)).start()
     for load in loads[4:7]:
         load.wait()
     advection(vel_ref, metric_ref, const_ref, table, wsum)
     azimuth_pairs(wsum, face_out)
+    pl.semaphore_wait(barrier, n_xs + 1)
+    for place in range(n_xs - 1, 0, -1):
+        query_copy(place, 1, place // GROUP, ahead(place)).start()
     for side in range(2):
         face_copy(side).start()
 

time: 27.7 us -> 28.2 us (1.018)
  Pallas kernels: 26.9 us -> 27.4 us
    pallas_call x1, Pallas kernels: 25.1 us -> 25.7 us  [shards(): pl.pallas_call(functools.partial(kernel, n_ax, n_xs), out_shape=outputs,...]
where the time goes in v6:
time: 28.2 us; the launch traced here: 28.1 us
  Pallas kernels  27.4 us (97%)
  between operations  0.64 us (2%)
    pallas_call x1, Pallas kernels, shards(): pl.pallas_call(functools.partial(kernel, n_ax, n_xs), out_shape=outputs,...  25.7 us
    pallas_call x1, Pallas kernels, shards(): pl.pallas_call(store, out_shape=outputs, in_specs=[anywhere, anywhere], o...  1.76 us

profile of v6, /device:TPU:1, one launch (start us, length us, event | category | flops | bytes accessed | tf_op | source)
XLA Modules:
  0.0 28.1 jit_solution(8900210591787178175)
XLA Ops:
  0.6 25.7 %shard_map.113 = (f32[3,8,32,128]{3,2,1,0:T(8,128)}, f32[3,1024]{1,0:T(4,128)}) custom-call(s32[1,1024]{1,0:T(1,128)} %bitcast.10, s32[1,1024]{1,0:T(1,128)} %bitcast.11, f32[3,1024]{1,0:T(4,128)} %ref_hbm.1, f32[1,1024]{1,0:T(1,128)} %bitcast.12, f32[3,8,32,128]{3,2,1,0:T(8,128)} %vel_hbm.1, f32[3,4,16]{2,1,0:T(4,128)} %bitcast.9, ...), custom_call_target="tpu_custom_call" | custom-call | tf_op jit(solution)/shard_map/pallas_call | solution.py:525
  26.3 1.8 %shard_map.114 = (f32[3,8,32,128]{3,2,1,0:T(8,128)}, f32[3,1024]{1,0:T(4,128)}) custom-call(f32[3,8,32,128]{3,2,1,0:T(8,128)} %get-tuple-element.4.fluid_in, f32[3,1024]{1,0:T(4,128)} %get-tuple-element.5.bubble_in), custom_call_target="tpu_custom_call" | custom-call | tf_op jit(solution)/shard_map/pallas_call | solution.py:557

commit v7 on v5

--- a/solution.py
+++ b/solution.py
@@ -435,7 +435,7 @@
 
     groups = n_xs // GROUP
     middle = groups // 4
-    order = list(range(middle, groups - 3))
+    order = list(range(middle, groups - 4))
     order += [g for g in range(groups - 1, -1, -1) if g not in order]
     for turn, group in enumerate(order):
         if turn == min(3, groups - 1):

time: 27.7 us -> 27.4 us (0.989)
  Pallas kernels: 26.9 us -> 26.6 us
where the time goes in v7:
time: 27.4 us; the launch traced here: 27.3 us
  Pallas kernels  26.6 us (97%)
  between operations  0.64 us (2%)
    pallas_call x1, Pallas kernels, shards(): pl.pallas_call(functools.partial(kernel, n_ax, n_xs), out_shape=outputs,...  24.9 us
    pallas_call x1, Pallas kernels, shards(): pl.pallas_call(store, out_shape=outputs, in_specs=[anywhere, anywhere], o...  1.76 us

profile of v7, /device:TPU:1, one launch (start us, length us, event | category | flops | bytes accessed | tf_op | source)
XLA Modules:
  0.0 27.3 jit_solution(2600817413312783543)
XLA Ops:
  0.6 24.9 %shard_map.113 = (f32[3,8,32,128]{3,2,1,0:T(8,128)}, f32[3,1024]{1,0:T(4,128)}) custom-call(s32[1,1024]{1,0:T(1,128)} %bitcast.10, s32[1,1024]{1,0:T(1,128)} %bitcast.11, f32[3,1024]{1,0:T(4,128)} %ref_hbm.1, f32[1,1024]{1,0:T(1,128)} %bitcast.12, f32[3,8,32,128]{3,2,1,0:T(8,128)} %vel_hbm.1, f32[3,4,16]{2,1,0:T(4,128)} %bitcast.9, ...), custom_call_target="tpu_custom_call" | custom-call | tf_op jit(solution)/shard_map/pallas_call | solution.py:525
  25.5 1.8 %shard_map.114 = (f32[3,8,32,128]{3,2,1,0:T(8,128)}, f32[3,1024]{1,0:T(4,128)}) custom-call(f32[3,8,32,128]{3,2,1,0:T(8,128)} %get-tuple-element.4.fluid_in, f32[3,1024]{1,0:T(4,128)} %get-tuple-element.5.bubble_in), custom_call_target="tpu_custom_call" | custom-call | tf_op jit(solution)/shard_map/pallas_call | solution.py:557
